TPU v7x, 32 devices: a whole 2x2x4 slice. The times are simulated.
32 devices in a mesh: seq: 16 (over z, x, core), head: 2 (over y).
Axes of the slice: x: 2, y: 2, z: 4, core: 2. Of those that a mesh axis runs over, the one named last changes fastest.
Arguments:
- queries: bfloat16 [4096, 32, 128], P('seq', 'head'), may hold values from -36 to 36
- keys: bfloat16 [4096, 16, 128], P('seq', 'head'), may hold values from -4 to 4
- values: bfloat16 [4096, 16, 128], P('seq', 'head'), may hold values from -12 to 12
- output_gradient: bfloat16 [4096, 32, 128], P('seq', 'head'), may hold values from -6 to 6
- segment_ids: int32 [4096], P('seq'), may hold values from 0 to 3, never falling along the last dimension, each value on 1 to 2048 neighbouring positions
- block_order: int32 [32], replicated, may hold values from 0 to 31, each once
Outputs:
- relaid: bfloat16 [4096, 4096], P(('seq', 'head'))
- query_grad: bfloat16 [4096, 32, 128], P('seq', 'head')
- key_grad: bfloat16 [4096, 16, 128], P('seq', 'head')
- value_grad: bfloat16 [4096, 16, 128], P('seq', 'head')
Inputs may be any that keep to these rules, and one draw needn't show every extreme that they name: `segment_ids`: segment ids never fall along the sequence; each document holds 1 to 2048 positions and one holds exactly 2048. `block_order`: each block number appears exactly once.
All inputs are finite; a program needn't handle non-finite values.
Results may differ from a plain program's by a relative error of at most 0.013.
Values may be sent and summed in bfloat16 or wider, within the bound.
A program may use at most 128 MiB of HBM per device.

v0:
```python
import jax
import jax.numpy as jnp
from jax import lax
from jax.sharding import PartitionSpec as P

WINDOW_LENGTH = 1024
QSCALAR = 168


def shifted(value, axis, by):
    count = lax.axis_size(axis)
    pairs = [(i, i + by) for i in range(count) if 0 <= i + by < count]
    return lax.ppermute(value, axis, pairs)


def attend_head(group_index, queries, output_gradient, window_kv, allowed, factor):
    group_width = queries.shape[1] // window_kv.shape[2]
    query_part = lax.dynamic_slice_in_dim(queries, group_index * group_width, group_width, 1)
    grad_part = lax.dynamic_slice_in_dim(output_gradient, group_index * group_width, group_width, 1)
    key_part = lax.dynamic_index_in_dim(window_kv[0], group_index, 1, keepdims=False)
    value_part = lax.dynamic_index_in_dim(window_kv[1], group_index, 1, keepdims=False)
    scores = (
        jnp.einsum("tgd,sd->gts", query_part, key_part, preferred_element_type=jnp.float32) * factor
    )
    masked = jnp.where(allowed, scores, -jnp.inf)
    row_max = jnp.max(masked, axis=2, keepdims=True)
    log_total = row_max + jnp.log(jnp.sum(jnp.exp(masked - row_max), axis=2, keepdims=True))
    weights = jnp.where(allowed, jnp.exp(scores - log_total), 0.0)
    probs = weights.astype(jnp.bfloat16)
    attended = jnp.einsum(
        "gts,sd->tgd", probs, value_part, preferred_element_type=jnp.float32
    ).astype(jnp.bfloat16)
    delta = jnp.sum(grad_part.astype(jnp.float32) * attended.astype(jnp.float32), axis=2)
    dprobs = jnp.einsum("tgd,sd->gts", grad_part, value_part, preferred_element_type=jnp.float32)
    score_grad = (weights * (dprobs - delta.T[:, :, None])).astype(jnp.bfloat16)
    query_grad = (
        factor * jnp.einsum("gts,sd->tgd", score_grad, key_part, preferred_element_type=jnp.float32)
    ).astype(jnp.bfloat16)
    key_grad = factor * jnp.einsum(
        "gts,tgd->sd", score_grad, query_part, preferred_element_type=jnp.float32
    )
    value_grad = jnp.einsum("gts,tgd->sd", probs, grad_part, preferred_element_type=jnp.float32)
    return (attended, log_total[:, :, 0].T, delta, query_grad, key_grad, value_grad)


def local(queries, keys, values, output_gradient, segment_ids, block_order):
    tok_count = queries.shape[0]
    q_heads = queries.shape[1]
    head_size = queries.shape[2]
    kv_heads = keys.shape[1]
    seq_count = lax.axis_size("seq")
    factor = QSCALAR ** (-0.5)
    reach_count = (WINDOW_LENGTH - 1) // tok_count + 1
    device = lax.axis_index("seq")
    anchor = device * tok_count
    positions = jnp.arange(tok_count, dtype=jnp.int32)
    query_pos = anchor + positions
    doc_count = tok_count * seq_count // WINDOW_LENGTH
    doc_ids = jnp.arange(doc_count, dtype=jnp.int32)
    member = segment_ids[:, None] == doc_ids[None, :]
    local_counts = jnp.sum(member.astype(jnp.int32), axis=0)
    doc_sizes = lax.psum(local_counts, "seq")
    doc_begins = jnp.cumsum(doc_sizes) - doc_sizes
    doc_start = jnp.sum(jnp.where(member, doc_begins[None, :], 0), axis=1)
    own_kv = jnp.stack([keys, values])
    nearby = [shifted(own_kv, "seq", distance) for distance in range(1, reach_count + 1)]
    window_kv = jnp.concatenate(nearby[::-1] + [own_kv], axis=1)
    key_pos = (
        anchor
        - reach_count * tok_count
        + jnp.arange((reach_count + 1) * tok_count, dtype=jnp.int32)
    )
    distance_grid = query_pos[:, None] - key_pos[None, :]
    allowed = (
        (distance_grid >= 0)
        & (distance_grid < WINDOW_LENGTH)
        & (key_pos[None, :] >= doc_start[:, None])
    )
    head_ids = jnp.arange(kv_heads, dtype=jnp.int32)

    def per_group(group_index):
        return attend_head(group_index, queries, output_gradient, window_kv, allowed, factor)

    attended_h, log_total, delta, query_grad_h, key_window, value_window = lax.map(
        per_group, head_ids
    )
    key_total = key_window[:, reach_count * tok_count :]
    value_total = value_window[:, reach_count * tok_count :]
    for distance in range(1, reach_count + 1):
        lower = (reach_count - distance) * tok_count
        partial_terms = jnp.stack(
            [key_window[:, lower : lower + tok_count], value_window[:, lower : lower + tok_count]]
        )
        returned = shifted(partial_terms, "seq", -distance)
        key_total = key_total + returned[0]
        value_total = value_total + returned[1]
    attended = jnp.moveaxis(attended_h, 0, 1).reshape(tok_count, q_heads, head_size)
    query_grad = jnp.moveaxis(query_grad_h, 0, 1).reshape(tok_count, q_heads, head_size)
    key_grad = jnp.moveaxis(key_total, 0, 1).astype(jnp.bfloat16)
    value_grad = jnp.moveaxis(value_total, 0, 1).astype(jnp.bfloat16)
    features = q_heads * head_size
    piece_rows = tok_count // 2 // seq_count
    flat_rows = attended.reshape(2, seq_count, piece_rows, features)
    spread_out = lax.all_to_all(flat_rows, "seq", split_axis=1, concat_axis=0, tiled=True)
    held_blocks = spread_out.reshape(2 * seq_count, piece_rows, features)
    ordered = jnp.take(held_blocks, block_order, axis=0)
    delivered = lax.all_to_all(
        ordered.reshape(seq_count, 2, 1, piece_rows, features),
        "seq",
        split_axis=0,
        concat_axis=2,
        tiled=True,
    )
    reordered = delivered.reshape(tok_count, features)
    relaid = lax.all_to_all(reordered, "head", split_axis=0, concat_axis=1, tiled=True)
    return (relaid, query_grad, key_grad, value_grad)


def solution(mesh):
    placed = (
        P("seq", "head", None),
        P("seq", "head", None),
        P("seq", "head", None),
        P("seq", "head", None),
        P("seq"),
        P(),
    )
    return jax.shard_map(
        local,
        mesh=mesh,
        in_specs=placed,
        out_specs=(
            P(("seq", "head"), None),
            P("seq", "head", None),
            P("seq", "head", None),
            P("seq", "head", None),
        ),
        check_vma=False,
    )
```

profile of v0, /device:TPU:8, one launch (start us, length us, event | category | flops | bytes accessed | tf_op | source)
XLA Modules:
  0.0 785.4 jit_solution(11455666846370291498)
XLA Ops:
  2.1 3.5 collective-permute-start
  5.6 2.6 collective-permute-start.1
  8.2 3.5 collective-permute-start.2
  11.7 2.6 collective-permute-start.3
  14.4 36.3 %psum.7 = s32[4]{0:T(128)S(1)} all-reduce(s32[4]{0:T(128)S(1)} %convert_reduce_fusion), channel_id=1, replica_groups=mesh['seq'=16,'head'=2] {'seq'}, use_global_device_ids=true, to_apply=%region_1.0 | all-reduce | flops 4 | bytes 32 | tf_op jit(solution)/shard_map/psum | solution.py:62
  54.3 21.7 %collective-permute-done.2 = bf16[2,256,8,128]{3,1,2,0:T(8,128)(2,1)} collective-permute-done((bf16[2,256,8,128]{3,1,2,0:T(8,128)(2,1)S(1)}, bf16[2,256,8,128]{3,1,2,0:T(8,128)(2,1)}, u32[]{:S(2)}, u32[]{:S(2)}) %collective-permute-start.2) | collective-permute-done | bytes 1048608 | tf_op jit(solution)/shard_map/ppermute | solution.py:13
  77.5 8.7 %collective-permute-done.3 = bf16[2,256,8,128]{3,1,2,0:T(8,128)(2,1)S(1)} collective-permute-done((bf16[2,256,8,128]{3,1,2,0:T(8,128)(2,1)S(1)}, bf16[2,256,8,128]{3,1,2,0:T(8,128)(2,1)S(1)}, u32[]{:S(2)}, u32[]{:S(2)}) %collective-permute-start.3) | collective-permute-done | bytes 1048608 | tf_op jit(solution)/shard_map/ppermute | solution.py:13
  87.1 1.6 copy-done
  88.7 456.4 %while.17 = (s32[]{:T(128)}, bf16[8,256,2,128]{1,3,2,0:T(8,128)(2,1)}, bf16[8,256,2,128]{1,3,2,0:T(8,128)(2,1)}, f32[8,1280,128]{2,0,1:T(8,128)}, f32[8,1280,128...) while((s32[]{:T(128)}, ...), condition=%wide.region_8.9_spmd.clone, body=%wide.region_4.8_spmd.clone.sunk | while | flops 1020361728 | bytes 59012472 | solution.py:84
  93.3 4.5 fusion.72
  100.6 2.5 bitcast_dynamic-update-slice_fusion.2
  103.4 2.6 fusion.73
  107.5 18.5 %dynamic_update_slice.26 = f32[8,1280,128]{2,0,1:T(8,128)} dynamic-update-slice(f32[8,1280,128]{2,0,1:T(8,128)} %get-tuple-element.329, f32[1,1280,128]{2,0,1:T(1,128)S(1)} %bitcast.206, s32[]{:T(128)S(6)} %copy.207, s32[]{:T(128)} %constant.60.clone.1..sunk, s32[]{:T(128)} %constant.60.clone.1..sunk) | dynamic-update-slice | bytes 1310724 | tf_op jit(solution)/shard_map/while/body/jit(dynamic_update_index_in_dim)/dynamic_update_slice | solution.py:84
  127.6 18.2 %dynamic_update_slice.27 = f32[8,1280,128]{2,0,1:T(8,128)} dynamic-update-slice(f32[8,1280,128]{2,0,1:T(8,128)} %get-tuple-element.330, f32[1,1280,128]{2,0,1:T(1,128)S(1)} %bitcast.207, s32[]{:T(128)S(6)} %copy.207, s32[]{:T(128)} %constant.60.clone.1..sunk, s32[]{:T(128)} %constant.60.clone.1..sunk) | dynamic-update-slice | bytes 1310724 | tf_op jit(solution)/shard_map/while/body/jit(dynamic_update_index_in_dim)/dynamic_update_slice | solution.py:84
  150.3 4.5 fusion.72
  157.7 2.5 bitcast_dynamic-update-slice_fusion.2
  160.4 2.6 fusion.73
  164.6 18.5 %dynamic_update_slice.26 = f32[8,1280,128]{2,0,1:T(8,128)} dynamic-update-slice(f32[8,1280,128]{2,0,1:T(8,128)} %get-tuple-element.329, f32[1,1280,128]{2,0,1:T(1,128)S(1)} %bitcast.206, s32[]{:T(128)S(6)} %copy.207, s32[]{:T(128)} %constant.60.clone.1..sunk, s32[]{:T(128)} %constant.60.clone.1..sunk) | dynamic-update-slice | bytes 1310724 | tf_op jit(solution)/shard_map/while/body/jit(dynamic_update_index_in_dim)/dynamic_update_slice | solution.py:84
  183.1 1.5 fusion.76
  184.6 18.2 %dynamic_update_slice.27 = f32[8,1280,128]{2,0,1:T(8,128)} dynamic-update-slice(f32[8,1280,128]{2,0,1:T(8,128)} %get-tuple-element.330, f32[1,1280,128]{2,0,1:T(1,128)S(1)} %bitcast.207, s32[]{:T(128)S(6)} %copy.207, s32[]{:T(128)} %constant.60.clone.1..sunk, s32[]{:T(128)} %constant.60.clone.1..sunk) | dynamic-update-slice | bytes 1310724 | tf_op jit(solution)/shard_map/while/body/jit(dynamic_update_index_in_dim)/dynamic_update_slice | solution.py:84
  207.3 4.5 fusion.72
  214.8 2.5 bitcast_dynamic-update-slice_fusion.2
  217.5 2.6 fusion.73
  221.7 18.5 %dynamic_update_slice.26 = f32[8,1280,128]{2,0,1:T(8,128)} dynamic-update-slice(f32[8,1280,128]{2,0,1:T(8,128)} %get-tuple-element.329, f32[1,1280,128]{2,0,1:T(1,128)S(1)} %bitcast.206, s32[]{:T(128)S(6)} %copy.207, s32[]{:T(128)} %constant.60.clone.1..sunk, s32[]{:T(128)} %constant.60.clone.1..sunk) | dynamic-update-slice | bytes 1310724 | tf_op jit(solution)/shard_map/while/body/jit(dynamic_update_index_in_dim)/dynamic_update_slice | solution.py:84
  241.7 18.2 %dynamic_update_slice.27 = f32[8,1280,128]{2,0,1:T(8,128)} dynamic-update-slice(f32[8,1280,128]{2,0,1:T(8,128)} %get-tuple-element.330, f32[1,1280,128]{2,0,1:T(1,128)S(1)} %bitcast.207, s32[]{:T(128)S(6)} %copy.207, s32[]{:T(128)} %constant.60.clone.1..sunk, s32[]{:T(128)} %constant.60.clone.1..sunk) | dynamic-update-slice | bytes 1310724 | tf_op jit(solution)/shard_map/while/body/jit(dynamic_update_index_in_dim)/dynamic_update_slice | solution.py:84
  264.4 4.5 fusion.72
  271.8 2.5 bitcast_dynamic-update-slice_fusion.2
  274.5 2.6 fusion.73
  278.7 18.5 %dynamic_update_slice.26 = f32[8,1280,128]{2,0,1:T(8,128)} dynamic-update-slice(f32[8,1280,128]{2,0,1:T(8,128)} %get-tuple-element.329, f32[1,1280,128]{2,0,1:T(1,128)S(1)} %bitcast.206, s32[]{:T(128)S(6)} %copy.207, s32[]{:T(128)} %constant.60.clone.1..sunk, s32[]{:T(128)} %constant.60.clone.1..sunk) | dynamic-update-slice | bytes 1310724 | tf_op jit(solution)/shard_map/while/body/jit(dynamic_update_index_in_dim)/dynamic_update_slice | solution.py:84
  298.7 18.2 %dynamic_update_slice.27 = f32[8,1280,128]{2,0,1:T(8,128)} dynamic-update-slice(f32[8,1280,128]{2,0,1:T(8,128)} %get-tuple-element.330, f32[1,1280,128]{2,0,1:T(1,128)S(1)} %bitcast.207, s32[]{:T(128)S(6)} %copy.207, s32[]{:T(128)} %constant.60.clone.1..sunk, s32[]{:T(128)} %constant.60.clone.1..sunk) | dynamic-update-slice | bytes 1310724 | tf_op jit(solution)/shard_map/while/body/jit(dynamic_update_index_in_dim)/dynamic_update_slice | solution.py:84
  321.5 4.5 fusion.72
  328.9 2.5 bitcast_dynamic-update-slice_fusion.2
  331.6 2.6 fusion.73
  335.8 18.5 %dynamic_update_slice.26 = f32[8,1280,128]{2,0,1:T(8,128)} dynamic-update-slice(f32[8,1280,128]{2,0,1:T(8,128)} %get-tuple-element.329, f32[1,1280,128]{2,0,1:T(1,128)S(1)} %bitcast.206, s32[]{:T(128)S(6)} %copy.207, s32[]{:T(128)} %constant.60.clone.1..sunk, s32[]{:T(128)} %constant.60.clone.1..sunk) | dynamic-update-slice | bytes 1310724 | tf_op jit(solution)/shard_map/while/body/jit(dynamic_update_index_in_dim)/dynamic_update_slice | solution.py:84
  355.8 18.2 %dynamic_update_slice.27 = f32[8,1280,128]{2,0,1:T(8,128)} dynamic-update-slice(f32[8,1280,128]{2,0,1:T(8,128)} %get-tuple-element.330, f32[1,1280,128]{2,0,1:T(1,128)S(1)} %bitcast.207, s32[]{:T(128)S(6)} %copy.207, s32[]{:T(128)} %constant.60.clone.1..sunk, s32[]{:T(128)} %constant.60.clone.1..sunk) | dynamic-update-slice | bytes 1310724 | tf_op jit(solution)/shard_map/while/body/jit(dynamic_update_index_in_dim)/dynamic_update_slice | solution.py:84
  378.5 4.5 fusion.72
  385.9 2.5 bitcast_dynamic-update-slice_fusion.2
  388.6 2.6 fusion.73
  392.8 18.5 %dynamic_update_slice.26 = f32[8,1280,128]{2,0,1:T(8,128)} dynamic-update-slice(f32[8,1280,128]{2,0,1:T(8,128)} %get-tuple-element.329, f32[1,1280,128]{2,0,1:T(1,128)S(1)} %bitcast.206, s32[]{:T(128)S(6)} %copy.207, s32[]{:T(128)} %constant.60.clone.1..sunk, s32[]{:T(128)} %constant.60.clone.1..sunk) | dynamic-update-slice | bytes 1310724 | tf_op jit(solution)/shard_map/while/body/jit(dynamic_update_index_in_dim)/dynamic_update_slice | solution.py:84
  411.3 1.5 fusion.76
  412.8 18.2 %dynamic_update_slice.27 = f32[8,1280,128]{2,0,1:T(8,128)} dynamic-update-slice(f32[8,1280,128]{2,0,1:T(8,128)} %get-tuple-element.330, f32[1,1280,128]{2,0,1:T(1,128)S(1)} %bitcast.207, s32[]{:T(128)S(6)} %copy.207, s32[]{:T(128)} %constant.60.clone.1..sunk, s32[]{:T(128)} %constant.60.clone.1..sunk) | dynamic-update-slice | bytes 1310724 | tf_op jit(solution)/shard_map/while/body/jit(dynamic_update_index_in_dim)/dynamic_update_slice | solution.py:84
  435.6 4.5 fusion.72
  443.0 2.5 bitcast_dynamic-update-slice_fusion.2
  445.7 2.6 fusion.73
  449.9 18.5 %dynamic_update_slice.26 = f32[8,1280,128]{2,0,1:T(8,128)} dynamic-update-slice(f32[8,1280,128]{2,0,1:T(8,128)} %get-tuple-element.329, f32[1,1280,128]{2,0,1:T(1,128)S(1)} %bitcast.206, s32[]{:T(128)S(6)} %copy.207, s32[]{:T(128)} %constant.60.clone.1..sunk, s32[]{:T(128)} %constant.60.clone.1..sunk) | dynamic-update-slice | bytes 1310724 | tf_op jit(solution)/shard_map/while/body/jit(dynamic_update_index_in_dim)/dynamic_update_slice | solution.py:84
  469.9 18.2 %dynamic_update_slice.27 = f32[8,1280,128]{2,0,1:T(8,128)} dynamic-update-slice(f32[8,1280,128]{2,0,1:T(8,128)} %get-tuple-element.330, f32[1,1280,128]{2,0,1:T(1,128)S(1)} %bitcast.207, s32[]{:T(128)S(6)} %copy.207, s32[]{:T(128)} %constant.60.clone.1..sunk, s32[]{:T(128)} %constant.60.clone.1..sunk) | dynamic-update-slice | bytes 1310724 | tf_op jit(solution)/shard_map/while/body/jit(dynamic_update_index_in_dim)/dynamic_update_slice | solution.py:84
  492.6 4.5 fusion.72
  500.0 2.5 bitcast_dynamic-update-slice_fusion.2
  502.7 2.6 fusion.73
  506.9 18.5 %dynamic_update_slice.26 = f32[8,1280,128]{2,0,1:T(8,128)} dynamic-update-slice(f32[8,1280,128]{2,0,1:T(8,128)} %get-tuple-element.329, f32[1,1280,128]{2,0,1:T(1,128)S(1)} %bitcast.206, s32[]{:T(128)S(6)} %copy.207, s32[]{:T(128)} %constant.60.clone.1..sunk, s32[]{:T(128)} %constant.60.clone.1..sunk) | dynamic-update-slice | bytes 1310724 | tf_op jit(solution)/shard_map/while/body/jit(dynamic_update_index_in_dim)/dynamic_update_slice | solution.py:84
  526.9 18.2 %dynamic_update_slice.27 = f32[8,1280,128]{2,0,1:T(8,128)} dynamic-update-slice(f32[8,1280,128]{2,0,1:T(8,128)} %get-tuple-element.330, f32[1,1280,128]{2,0,1:T(1,128)S(1)} %bitcast.207, s32[]{:T(128)S(6)} %copy.207, s32[]{:T(128)} %constant.60.clone.1..sunk, s32[]{:T(128)} %constant.60.clone.1..sunk) | dynamic-update-slice | bytes 1310724 | tf_op jit(solution)/shard_map/while/body/jit(dynamic_update_index_in_dim)/dynamic_update_slice | solution.py:84
  545.1 2.6 copy.147
  549.6 11.2 %all-to-all-start = ((bf16[2,16,8,2048]{3,2,0,1:T(8,128)(2,1)}), bf16[2,16,8,2048]{3,2,0,1:T(8,128)(2,1)S(1)}, u32[]{:S(2)}, u32[]{:S(2)}) async-start(bf16[2,16,8,2048]{3,2,0,1:T(8,128)(2,1)} %copy.148), calls=%async_computation | async-start | bytes 2097152 | tf_op jit(solution)/shard_map/all_to_all | solution.py:104
  560.9 2.6 slice_bitcast_fusion.14
  566.1 2.0 collective-permute-start.7
  569.6 1.9 collective-permute-start.6
  573.1 2.0 collective-permute-start.5
  576.5 2.4 collective-permute-start.4
  578.9 6.3 all-to-all-done
  586.0 178.1 %all_to_all.49 = bf16[16,2,1,8,2048]{4,3,1,2,0:T(8,128)(2,1)S(1)} all-to-all(bf16[16,2,1,8,2048]{4,3,1,2,0:T(8,128)(2,1)S(1)} %select_bitcast_fusion), channel_id=1, replica_groups=mesh['seq'=16,'head'=2] {'seq'}, dimensions={0} | all-to-all | bytes 2097152 | tf_op jit(solution)/shard_map/all_to_all | solution.py:107
  765.1 3.6 all-to-all-start.2
  768.7 2.1 copy.152
  770.8 5.4 fusion.43
  776.2 7.2 all-to-all-done.2
  (186 shorter events, 82.8 us)
Async XLA Ops:
  0.6 13.7 %copy-start.5 = (s32[256]{0:T(256)S(1)}, s32[256]{0:T(256)}, u32[]{:S(2)}) copy-start(s32[256]{0:T(256)} %param.12) | copy-start | bytes 3076
  2.1 49.5 %collective-permute-start = (bf16[2,256,8,128]{3,1,2,0:T(8,128)(2,1)S(1)}, bf16[2,256,8,128]{3,1,2,0:T(8,128)(2,1)}, u32[]{:S(2)}, u32[]{:S(2)}) collective-permute-start(bf16[2,256,8,128]{3,1,2,0:T(8,128)(2,1)S(1)} %pad_maximum_fusion.4), channel_id=1, source_target_pairs={{0,8},{2,10},{4,12},{6,14},{8,16},{10,18},{12,20},{14,22},{16,24},... | collective-permute-start | bytes 3145736 | tf_op jit(solution)/shard_map/ppermute | solution.py:13
  5.6 47.3 %collective-permute-start.1 = (bf16[2,256,8,128]{3,1,2,0:T(8,128)(2,1)S(1)}, bf16[2,256,8,128]{3,1,2,0:T(8,128)(2,1)}, u32[]{:S(2)}, u32[]{:S(2)}) collective-permute-start(bf16[2,256,8,128]{3,1,2,0:T(8,128)(2,1)S(1)} %pad_maximum_fusion.4), channel_id=1, source_target_pairs={{0,6},{2,8},{4,10},{6,12},{8,14},{10,16},{12,18},{14,20},{16,22},{... | collective-permute-start | bytes 3145736 | tf_op jit(solution)/shard_map/ppermute | solution.py:13
  8.2 67.9 %collective-permute-start.2 = (bf16[2,256,8,128]{3,1,2,0:T(8,128)(2,1)S(1)}, bf16[2,256,8,128]{3,1,2,0:T(8,128)(2,1)}, u32[]{:S(2)}, u32[]{:S(2)}) collective-permute-start(bf16[2,256,8,128]{3,1,2,0:T(8,128)(2,1)S(1)} %pad_maximum_fusion.4), channel_id=1, source_target_pairs={{0,4},{2,6},{4,8},{6,10},{8,12},{10,14},{12,16},{14,18},{16,20},{1... | collective-permute-start | bytes 3145736 | tf_op jit(solution)/shard_map/ppermute | solution.py:13
  11.7 74.5 %collective-permute-start.3 = (bf16[2,256,8,128]{3,1,2,0:T(8,128)(2,1)S(1)}, bf16[2,256,8,128]{3,1,2,0:T(8,128)(2,1)S(1)}, u32[]{:S(2)}, u32[]{:S(2)}) collective-permute-start(bf16[2,256,8,128]{3,1,2,0:T(8,128)(2,1)S(1)} %pad_maximum_fusion.4), channel_id=1, source_target_pairs={{0,2},{2,4},{4,6},{6,8},{8,10},{10,12},{12,14},{14,16},{16,18},{18... | collective-permute-start | bytes 3145736 | tf_op jit(solution)/shard_map/ppermute | solution.py:13
  86.4 2.3 copy-start
  89.8 13.5 %copy-start.3 = (pred[256,1280]{0,1:T(8,128)(4,1)}, pred[256,1280]{0,1:T(8,128)(4,1)S(1)}, u32[]{:S(2)}) copy-start(pred[256,1280]{0,1:T(8,128)(4,1)S(1)} %fusion.71) | copy-start | bytes 983044 | tf_op jit(solution)/shard_map/while
  100.1 3.1 copy-start.1
  107.0 19.0 %copy-start.2 = (f32[2,256,1280]{1,2,0:T(8,128)S(1)}, f32[2,256,1280]{1,2,0:T(8,128)}, u32[]{:S(2)}) copy-start(f32[2,256,1280]{1,2,0:T(8,128)} %copy-done.1) | copy-start | bytes 7864324 | tf_op jit(solution)/shard_map/while
  146.9 13.5 %copy-start.3 = (pred[256,1280]{0,1:T(8,128)(4,1)}, pred[256,1280]{0,1:T(8,128)(4,1)S(1)}, u32[]{:S(2)}) copy-start(pred[256,1280]{0,1:T(8,128)(4,1)S(1)} %fusion.71) | copy-start | bytes 983044 | tf_op jit(solution)/shard_map/while
  157.1 3.1 copy-start.1
  164.1 19.0 %copy-start.2 = (f32[2,256,1280]{1,2,0:T(8,128)S(1)}, f32[2,256,1280]{1,2,0:T(8,128)}, u32[]{:S(2)}) copy-start(f32[2,256,1280]{1,2,0:T(8,128)} %copy-done.1) | copy-start | bytes 7864324 | tf_op jit(solution)/shard_map/while
  203.9 13.5 %copy-start.3 = (pred[256,1280]{0,1:T(8,128)(4,1)}, pred[256,1280]{0,1:T(8,128)(4,1)S(1)}, u32[]{:S(2)}) copy-start(pred[256,1280]{0,1:T(8,128)(4,1)S(1)} %fusion.71) | copy-start | bytes 983044 | tf_op jit(solution)/shard_map/while
  214.2 3.1 copy-start.1
  221.1 19.0 %copy-start.2 = (f32[2,256,1280]{1,2,0:T(8,128)S(1)}, f32[2,256,1280]{1,2,0:T(8,128)}, u32[]{:S(2)}) copy-start(f32[2,256,1280]{1,2,0:T(8,128)} %copy-done.1) | copy-start | bytes 7864324 | tf_op jit(solution)/shard_map/while
  261.0 13.5 %copy-start.3 = (pred[256,1280]{0,1:T(8,128)(4,1)}, pred[256,1280]{0,1:T(8,128)(4,1)S(1)}, u32[]{:S(2)}) copy-start(pred[256,1280]{0,1:T(8,128)(4,1)S(1)} %fusion.71) | copy-start | bytes 983044 | tf_op jit(solution)/shard_map/while
  271.2 3.1 copy-start.1
  278.2 19.0 %copy-start.2 = (f32[2,256,1280]{1,2,0:T(8,128)S(1)}, f32[2,256,1280]{1,2,0:T(8,128)}, u32[]{:S(2)}) copy-start(f32[2,256,1280]{1,2,0:T(8,128)} %copy-done.1) | copy-start | bytes 7864324 | tf_op jit(solution)/shard_map/while
  318.0 13.5 %copy-start.3 = (pred[256,1280]{0,1:T(8,128)(4,1)}, pred[256,1280]{0,1:T(8,128)(4,1)S(1)}, u32[]{:S(2)}) copy-start(pred[256,1280]{0,1:T(8,128)(4,1)S(1)} %fusion.71) | copy-start | bytes 983044 | tf_op jit(solution)/shard_map/while
  328.3 3.1 copy-start.1
  335.2 19.0 %copy-start.2 = (f32[2,256,1280]{1,2,0:T(8,128)S(1)}, f32[2,256,1280]{1,2,0:T(8,128)}, u32[]{:S(2)}) copy-start(f32[2,256,1280]{1,2,0:T(8,128)} %copy-done.1) | copy-start | bytes 7864324 | tf_op jit(solution)/shard_map/while
  375.1 13.5 %copy-start.3 = (pred[256,1280]{0,1:T(8,128)(4,1)}, pred[256,1280]{0,1:T(8,128)(4,1)S(1)}, u32[]{:S(2)}) copy-start(pred[256,1280]{0,1:T(8,128)(4,1)S(1)} %fusion.71) | copy-start | bytes 983044 | tf_op jit(solution)/shard_map/while
  385.4 3.1 copy-start.1
  392.3 19.0 %copy-start.2 = (f32[2,256,1280]{1,2,0:T(8,128)S(1)}, f32[2,256,1280]{1,2,0:T(8,128)}, u32[]{:S(2)}) copy-start(f32[2,256,1280]{1,2,0:T(8,128)} %copy-done.1) | copy-start | bytes 7864324 | tf_op jit(solution)/shard_map/while
  432.2 13.5 %copy-start.3 = (pred[256,1280]{0,1:T(8,128)(4,1)}, pred[256,1280]{0,1:T(8,128)(4,1)S(1)}, u32[]{:S(2)}) copy-start(pred[256,1280]{0,1:T(8,128)(4,1)S(1)} %fusion.71) | copy-start | bytes 983044 | tf_op jit(solution)/shard_map/while
  442.4 3.1 copy-start.1
  449.4 19.0 %copy-start.2 = (f32[2,256,1280]{1,2,0:T(8,128)S(1)}, f32[2,256,1280]{1,2,0:T(8,128)}, u32[]{:S(2)}) copy-start(f32[2,256,1280]{1,2,0:T(8,128)} %copy-done.1) | copy-start | bytes 7864324 | tf_op jit(solution)/shard_map/while
  489.2 13.5 %copy-start.3 = (pred[256,1280]{0,1:T(8,128)(4,1)}, pred[256,1280]{0,1:T(8,128)(4,1)S(1)}, u32[]{:S(2)}) copy-start(pred[256,1280]{0,1:T(8,128)(4,1)S(1)} %fusion.71) | copy-start | bytes 983044 | tf_op jit(solution)/shard_map/while
  499.5 3.1 copy-start.1
  506.4 19.0 %copy-start.2 = (f32[2,256,1280]{1,2,0:T(8,128)S(1)}, f32[2,256,1280]{1,2,0:T(8,128)}, u32[]{:S(2)}) copy-start(f32[2,256,1280]{1,2,0:T(8,128)} %copy-done.1) | copy-start | bytes 7864324 | tf_op jit(solution)/shard_map/while
  548.5 12.3 %copy-start.6 = (s32[32]{0:T(128)S(1)}, s32[32]{0:T(128)}, u32[]{:S(2)}) copy-start(s32[32]{0:T(128)} %param.13) | copy-start | bytes 388
  549.6 14.0 %slice-start = ((s8[5242880]{0:T(1024)(128)(4,1)}), s8[1048576]{0:T(1024)(128)(4,1)S(1)}, s32[]{:S(2)}) async-start(s8[5242880]{0:T(1024)(128)(4,1)} %bitcast.208), calls=%async_computation.3 | async-start | bytes 2097152
  549.6 35.6 %all-to-all-start = ((bf16[2,16,8,2048]{3,2,0,1:T(8,128)(2,1)}), bf16[2,16,8,2048]{3,2,0,1:T(8,128)(2,1)S(1)}, u32[]{:S(2)}, u32[]{:S(2)}) async-start(bf16[2,16,8,2048]{3,2,0,1:T(8,128)(2,1)} %copy.148), calls=%async_computation | async-start | bytes 2097152 | tf_op jit(solution)/shard_map/all_to_all | solution.py:104
  560.9 3.5 slice-start.1
  566.1 204.6 %collective-permute-start.7 = (f32[2,8,256,128]{3,1,2,0:T(8,128)}, f32[2,8,256,128]{3,1,2,0:T(8,128)}, u32[]{:S(2)}, u32[]{:S(2)}) collective-permute-start(f32[2,8,256,128]{3,1,2,0:T(8,128)} %pad_maximum_fusion.3), channel_id=1, source_target_pairs={{8,0},{10,2},{12,4},{14,6},{16,8},{18,10},{20,12},{22,14},{24,16},... | collective-permute-start | bytes 6291464 | tf_op jit(solution)/shard_map/ppermute | solution.py:13
  569.6 201.1 %collective-permute-start.6 = (f32[2,8,256,128]{3,1,2,0:T(8,128)}, f32[2,8,256,128]{3,1,2,0:T(8,128)}, u32[]{:S(2)}, u32[]{:S(2)}) collective-permute-start(f32[2,8,256,128]{3,1,2,0:T(8,128)} %pad_maximum_fusion.2), channel_id=1, source_target_pairs={{6,0},{8,2},{10,4},{12,6},{14,8},{16,10},{18,12},{20,14},{22,16},{... | collective-permute-start | bytes 6291464 | tf_op jit(solution)/shard_map/ppermute | solution.py:13
  573.1 197.7 %collective-permute-start.5 = (f32[2,8,256,128]{3,1,2,0:T(8,128)}, f32[2,8,256,128]{3,1,2,0:T(8,128)}, u32[]{:S(2)}, u32[]{:S(2)}) collective-permute-start(f32[2,8,256,128]{3,1,2,0:T(8,128)} %pad_maximum_fusion.1), channel_id=1, source_target_pairs={{4,0},{6,2},{8,4},{10,6},{12,8},{14,10},{16,12},{18,14},{20,16},{2... | collective-permute-start | bytes 6291464 | tf_op jit(solution)/shard_map/ppermute | solution.py:13
  576.5 194.2 %collective-permute-start.4 = (f32[2,8,256,128]{3,1,2,0:T(8,128)}, f32[2,8,256,128]{3,1,2,0:T(8,128)}, u32[]{:S(2)}, u32[]{:S(2)}) collective-permute-start(f32[2,8,256,128]{3,1,2,0:T(8,128)} %pad_maximum_fusion), channel_id=1, source_target_pairs={{2,0},{4,2},{6,4},{8,6},{10,8},{12,10},{14,12},{16,14},{18,16},{20... | collective-permute-start | bytes 6291464 | tf_op jit(solution)/shard_map/ppermute | solution.py:13
  764.0 4.6 copy-start.4
  765.1 18.3 %all-to-all-start.2 = ((bf16[2,128,2048]{2,1,0:T(8,128)(2,1)}), bf16[2,128,2048]{2,1,0:T(8,128)(2,1)S(1)}, u32[]{:S(2)}, u32[]{:S(2)}) async-start(bf16[2,128,2048]{2,1,0:T(8,128)(2,1)} %bitcast.171), calls=%async_computation.2 | async-start | bytes 2097152 | tf_op jit(solution)/shard_map/all_to_all | solution.py:115
where the time goes:
time: 796 us; the launch traced here: 785 us
  local copies, waits for them, and re-layouts  374 us (47%)
  blocking collectives  214 us (27%)
  matrix products  70.1 us (9%)
  waiting for transfers between devices  43.9 us (6%)
  starting transfers between devices  35.2 us (4%)
  other arithmetic  26.5 us (3%)
  loops' own time  20.6 us (3%)
    dynamic_update_slice x16, local copies, waits for them, and re-layouts, local(): lax.map(per_group, head_ids)  293 us
    all_to_all x1, blocking collectives, local(): lax.all_to_all(ordered.reshape(seq_count, 2, 1, piece_rows, features), 's...  178 us
    psum x1, blocking collectives, local(): doc_sizes = lax.psum(local_counts, 'seq')  36.3 us
    slice x8, local copies, waits for them, and re-layouts, attend_head(): window_kv[0]  35.6 us
    ppermute x8, waiting for transfers between devices, shifted(): return lax.ppermute(value, axis, pairs)  30.4 us
    dot_general x8, matrix products, attend_head(): jnp.einsum('tgd,sd->gts', grad_part, value_part, preferred_element_type=j...  20.9 us
    another operation x1, loops' own time, local(): lax.map(per_group, head_ids)  20.6 us
    ppermute x8, starting transfers between devices, shifted(): return lax.ppermute(value, axis, pairs)  20.4 us
  transfers between devices with their start and end apart: 10, of which 4 were waited for; matrix products, arithmetic and copies ran while one was open for 3% of the time, Pallas kernels for 0%

commit v1 on v0

v1 whole, which is shorter than its diff:
```python
import functools

import jax
import jax.numpy as jnp
from jax import lax
from jax.experimental import pallas as pl
from jax.experimental.pallas import tpu as pltpu
from jax.sharding import PartitionSpec as P

WINDOW_LENGTH = 1024
QSCALAR = 168
FACTOR = QSCALAR ** (-0.5)
LOG2E = 1.4426950408889634
SEG_ROWS = 16


def shifted(value, axis, by):
    count = lax.axis_size(axis)
    pairs = [(i, i + by) for i in range(count) if 0 <= i + by < count]
    return lax.ppermute(value, axis, pairs)


def dot(a, b, ca, cb):
    return lax.dot_general(a, b, (((ca,), (cb,)), ((), ())), preferred_element_type=jnp.float32)


def attention_kernel(count, *refs):
    q_ref, do_ref, bias_ref = refs[:3]
    k_refs = refs[3 : 3 + count]
    v_refs = refs[3 + count : 3 + 2 * count]
    o_ref, dq_ref = refs[3 + 2 * count : 5 + 2 * count]
    g_refs = refs[5 + 2 * count : 5 + 3 * count]
    p_scr = refs[5 + 3 * count]
    width, tok, dim = q_ref.shape
    rows = width * tok
    q = q_ref[...].reshape(rows, dim)
    do = do_ref[...].reshape(rows, dim)
    top = None
    for b in range(count):
        s = dot(q, k_refs[b][...], 1, 1).reshape(width, tok, tok)
        s = (s + bias_ref[:, b * tok : (b + 1) * tok][None]).reshape(rows, tok)
        p_scr[b] = s
        m = jnp.max(s, axis=1, keepdims=True)
        top = m if top is None else jnp.maximum(top, m)
    total = jnp.zeros((rows, 1), jnp.float32)
    for b in range(count):
        p = jnp.exp2((p_scr[b] - top) * (FACTOR * LOG2E))
        p_scr[b] = p
        total += jnp.sum(p, axis=1, keepdims=True)
    scale = 1.0 / total
    out = jnp.zeros((rows, dim), jnp.float32)
    for b in range(count):
        w = p_scr[b] * scale
        p_scr[b] = w
        probs = w.astype(jnp.bfloat16)
        out += dot(probs, v_refs[b][...], 1, 0)
        g_refs[b][1, 0] = dot(probs, do, 0, 0).astype(g_refs[b].dtype)
    out = out.astype(jnp.bfloat16)
    for w in range(width):
        o_ref[:, w * dim : (w + 1) * dim] = out[w * tok : (w + 1) * tok]
    delta = jnp.sum(do.astype(jnp.float32) * out.astype(jnp.float32), axis=1, keepdims=True)
    dq = jnp.zeros((rows, dim), jnp.float32)
    for b in range(count):
        dp = dot(do, v_refs[b][...], 1, 1)
        ds = (p_scr[b] * (dp - delta)).astype(jnp.bfloat16)
        dq += dot(ds, k_refs[b][...], 1, 0)
        g_refs[b][0, 0] = (FACTOR * dot(ds, q, 0, 0)).astype(g_refs[b].dtype)
    dq_ref[...] = (FACTOR * dq).astype(jnp.bfloat16).reshape(width, tok, dim)


def attention(q, do, bias, windows):
    heads, tok, dim = q.shape
    count = len(windows)
    kv_heads = (windows[0].shape[0] - SEG_ROWS) // (2 * tok)
    width = heads // kv_heads
    head_spec = pl.BlockSpec((width, tok, dim), lambda h: (h, 0, 0))
    key_spec = pl.BlockSpec((tok, dim), lambda h: (h, 0))
    value_spec = pl.BlockSpec((tok, dim), lambda h: (h + kv_heads, 0))
    grad_spec = pl.BlockSpec((2, 1, tok, dim), lambda h: (0, h, 0, 0))
    grad_shape = (2, kv_heads, tok, dim)
    pairs = heads * tok * tok * count
    return pl.pallas_call(
        functools.partial(attention_kernel, count),
        grid=(kv_heads,),
        in_specs=[head_spec, head_spec, pl.BlockSpec((tok, count * tok), lambda h: (0, 0))]
        + [key_spec] * count
        + [value_spec] * count,
        out_specs=[pl.BlockSpec((tok, width * dim), lambda h: (0, h)), head_spec]
        + [grad_spec] * count,
        out_shape=[
            jax.ShapeDtypeStruct((tok, heads * dim), jnp.bfloat16),
            jax.ShapeDtypeStruct((heads, tok, dim), jnp.bfloat16),
        ]
        + [jax.ShapeDtypeStruct(grad_shape, jnp.bfloat16)] * (count - 1)
        + [jax.ShapeDtypeStruct(grad_shape, jnp.float32)],
        scratch_shapes=[pltpu.VMEM((count, width * tok, tok), jnp.float32)],
        compiler_params=pltpu.CompilerParams(vmem_limit_bytes=40 * 2**20),
        cost_estimate=pl.CostEstimate(
            flops=10 * pairs * dim, bytes_accessed=12 * 2**20, transcendentals=pairs
        ),
        name="attention",
    )(q, do, bias, *windows, *windows)


def pick_kernel(order_ref, held_ref, out_ref):
    for q in range(out_ref.shape[0]):
        out_ref[q] = held_ref[order_ref[q]]


def pick(held, order):
    return pl.pallas_call(
        pick_kernel,
        in_specs=[
            pl.BlockSpec(memory_space=pltpu.SMEM),
            pl.BlockSpec(memory_space=pltpu.VMEM),
        ],
        out_specs=pl.BlockSpec(memory_space=pltpu.VMEM),
        out_shape=jax.ShapeDtypeStruct(held.shape, held.dtype),
        name="pick",
    )(order, held)


def local(queries, keys, values, output_gradient, segment_ids, block_order):
    tok, q_heads, dim = queries.shape
    kv_heads = keys.shape[1]
    seq_count = lax.axis_size("seq")
    head_count = lax.axis_size("head")
    reach = (WINDOW_LENGTH - 1) // tok + 1
    anchor = lax.axis_index("seq") * tok

    seg_rows = segment_ids.astype(jnp.bfloat16).reshape(tok // dim, dim)
    own = jnp.concatenate(
        [
            jnp.moveaxis(keys, 1, 0).reshape(kv_heads * tok, dim),
            jnp.moveaxis(values, 1, 0).reshape(kv_heads * tok, dim),
            jnp.pad(seg_rows, ((0, SEG_ROWS - tok // dim), (0, 0))),
        ]
    )
    windows = [shifted(own, "seq", d) for d in range(reach, 0, -1)] + [own]
    base = 2 * kv_heads * tok
    key_segs = jnp.concatenate([w[base : base + tok // dim].reshape(tok) for w in windows])
    query_pos = anchor + jnp.arange(tok, dtype=jnp.int32)
    key_pos = anchor - reach * tok + jnp.arange((reach + 1) * tok, dtype=jnp.int32)
    distance = query_pos[:, None] - key_pos[None, :]
    allowed = (
        (distance >= 0)
        & (distance < WINDOW_LENGTH)
        & (key_pos[None, :] >= 0)
        & (segment_ids.astype(jnp.bfloat16)[:, None] == key_segs[None, :])
    )
    bias = jnp.where(allowed, 0.0, -jnp.inf).astype(jnp.float32)

    attended, dq, *grads = attention(
        jnp.moveaxis(queries, 1, 0), jnp.moveaxis(output_gradient, 1, 0), bias, windows
    )

    nb = block_order.shape[0] // seq_count
    piece = tok // nb // seq_count
    features = q_heads * dim
    flat = jnp.swapaxes(attended.reshape(nb, seq_count, piece, features), 0, 1)
    spread = lax.all_to_all(flat, "seq", split_axis=0, concat_axis=0, tiled=True)
    ordered = pick(spread.reshape(nb * seq_count, piece, features), block_order)
    delivered = lax.all_to_all(
        ordered.reshape(seq_count, nb, piece, features),
        "seq",
        split_axis=0,
        concat_axis=0,
        tiled=True,
    )
    reordered = jnp.swapaxes(delivered, 0, 1).reshape(head_count, tok // head_count, features)
    halves = lax.all_to_all(reordered, "head", split_axis=0, concat_axis=0, tiled=True)
    relaid = jnp.swapaxes(halves, 0, 1).reshape(tok // head_count, head_count * features)

    total = grads[reach]
    for d in range(1, reach + 1):
        total = total + shifted(grads[reach - d], "seq", -d).astype(jnp.float32)
    total = jnp.swapaxes(total, 1, 2).astype(jnp.bfloat16)
    return (relaid, jnp.moveaxis(dq, 0, 1), total[0], total[1])


def solution(mesh):
    placed = (
        P("seq", "head", None),
        P("seq", "head", None),
        P("seq", "head", None),
        P("seq", "head", None),
        P("seq"),
        P(),
    )
    return jax.shard_map(
        local,
        mesh=mesh,
        in_specs=placed,
        out_specs=(
            P(("seq", "head"), None),
            P("seq", "head", None),
            P("seq", "head", None),
            P("seq", "head", None),
        ),
        check_vma=False,
    )
```

time: 796 us -> 273 us (0.34); the launches traced: 785 us -> 273 us
  local copies, waits for them, and re-layouts: 374 us -> 16.9 us
  blocking collectives: 214 us -> 39.7 us
  waiting for transfers between devices: 43.9 us -> 144 us
  matrix products: 70.1 us -> 0 us
  Pallas kernels: 0 us -> 34.3 us
  loops' own time: 20.6 us -> 0 us
  other arithmetic: 26.5 us -> 6.03 us
    dynamic_update_slice x16 -> x0, local copies, waits for them, and re-layouts: 293 us -> none  [local(): lax.map(per_group, head_ids)]
    all_to_all x1, blocking collectives: 178 us -> 39.7 us  [local(): lax.all_to_all(flat, 'seq', split_axis=0, concat_axis=0, tiled=True)]
    ppermute x8, waiting for transfers between devices: 30.4 us -> 131 us  [shifted(): return lax.ppermute(value, axis, pairs)]
    dot_general x48 -> x0, matrix products: 70.1 us -> none  [the longest x8 20.9 us: attend_head(): jnp.einsum('tgd,sd->gts', grad_part, value_part, preferred_element_type=j...]
    psum x1 -> x0, blocking collectives: 36.3 us -> none  [local(): doc_sizes = lax.psum(local_counts, 'seq')]
    slice x8 -> x0, local copies, waits for them, and re-layouts: 35.6 us -> none  [attend_head(): window_kv[0]]
    pallas_call x0 -> x2, Pallas kernels: none -> 34.3 us  [the longest x1 32 us: attention(): pl.pallas_call(functools.partial(attention_kernel, count), grid=(kv_heads...]
    dynamic_slice x24 -> x0, local copies, waits for them, and re-layouts: 22.9 us -> none  [the longest x16 12.7 us: attend_head(): lax.dynamic_slice_in_dim(output_gradient, group_index * group_width, grou...]
  transfers between devices with their start and end apart: 10 -> 10, of which waited for: 4 -> 8; matrix products, arithmetic and copies ran while one was open for 3% -> 6% of each run, Pallas kernels for 0% -> 0%
where the time goes in v1:
time: 273 us
  waiting for transfers between devices  144 us (53%)
  blocking collectives  39.7 us (15%)
  Pallas kernels  34.3 us (13%)
  starting transfers between devices  30.4 us (11%)
  local copies, waits for them, and re-layouts  16.9 us (6%)
  other arithmetic  6.03 us (2%)
    ppermute x8, waiting for transfers between devices, shifted(): return lax.ppermute(value, axis, pairs)  131 us
    all_to_all x1, blocking collectives, local(): lax.all_to_all(flat, 'seq', split_axis=0, concat_axis=0, tiled=True)  39.7 us
    pallas_call x1, Pallas kernels, attention(): pl.pallas_call(functools.partial(attention_kernel, count), grid=(kv_heads...  32 us
    ppermute x8, starting transfers between devices, shifted(): return lax.ppermute(value, axis, pairs)  21.8 us
    all_to_all x1, waiting for transfers between devices, local(): lax.all_to_all(ordered.reshape(seq_count, nb, piece, features), 'seq', sp...  13.5 us
    unnamed x28, local copies, waits for them, and re-layouts  7.2 us
  transfers between devices with their start and end apart: 10, of which 8 were waited for; matrix products, arithmetic and copies ran while one was open for 6% of the time, Pallas kernels for 0%

profile of v1, /device:TPU:8, one launch (start us, length us, event | category | flops | bytes accessed | tf_op | source)
XLA Modules:
  0.0 272.6 jit_solution(6185156427641166856)
XLA Ops:
  0.6 0.0 copy-start.8
  0.6 0.7 convert_bitcast_fusion
  1.4 1.1 copy.40
  2.5 0.0 copy-done.8
  2.5 0.1 copy.41
  2.6 0.0 copy-start.9
  2.6 0.0 copy-start.7
  2.6 0.1 fusion.5.refs_7_.refs_12_
  2.7 3.6 %collective-permute-start = (bf16[4112,128]{1,0:T(8,128)(2,1)S(1)}, bf16[4112,128]{1,0:T(8,128)(2,1)}, u32[]{:S(2)}, u32[]{:S(2)}) collective-permute-start(bf16[4112,128]{1,0:T(8,128)(2,1)S(1)} %fusion.5.refs_7_.refs_12_), channel_id=1, source_target_pairs={{0,8},{2,10},{4,12},{6,14},{8,16},{10,18},{12,20},{14,22},{16,24},... | collective-permute-start | bytes 3158024 | tf_op jit(solution)/shard_map/ppermute | solution.py:20
  6.3 2.6 collective-permute-start.1
  8.9 3.0 %collective-permute-start.3 = (bf16[4112,128]{1,0:T(8,128)(2,1)S(1)}, bf16[4112,128]{1,0:T(8,128)(2,1)}, u32[]{:S(2)}, u32[]{:S(2)}) collective-permute-start(bf16[4112,128]{1,0:T(8,128)(2,1)S(1)} %fusion.5.refs_7_.refs_12_), channel_id=1, source_target_pairs={{0,2},{2,4},{4,6},{6,8},{8,10},{10,12},{12,14},{14,16},{16,18},{18... | collective-permute-start | bytes 3158024 | tf_op jit(solution)/shard_map/ppermute | solution.py:20
  11.8 3.4 %collective-permute-start.2 = (bf16[4112,128]{1,0:T(8,128)(2,1)S(1)}, bf16[4112,128]{1,0:T(8,128)(2,1)}, u32[]{:S(2)}, u32[]{:S(2)}) collective-permute-start(bf16[4112,128]{1,0:T(8,128)(2,1)S(1)} %fusion.5.refs_7_.refs_12_), channel_id=1, source_target_pairs={{0,4},{2,6},{4,8},{6,10},{8,12},{10,14},{12,16},{14,18},{16,20},{1... | collective-permute-start | bytes 3158024 | tf_op jit(solution)/shard_map/ppermute | solution.py:20
  15.3 0.0 copy-done.9
  15.3 0.0 copy-done.7
  15.3 2.7 %copy_bitcast_fusion.2 = (bf16[16,256,128]{2,1,0:T(8,128)(2,1)S(1)}, bf16[16,256,128]{2,1,0:T(8,128)(2,1)}) fusion(bf16[256,16,128]{2,1,0:T(8,128)(2,1)S(1)} %copy-done.7, bf16[256,16,128]{2,1,0:T(8,128)(2,1)} %param.6), kind=kLoop, calls=%fused_computation.13 | loop fusion | bytes 4194304 | tf_op jit(solution)/shard_map/transpose | solution.py:154
  18.1 12.9 %collective-permute-done.refs_3_.refs_8_ = bf16[4112,128]{1,0:T(8,128)(2,1)} collective-permute-done((bf16[4112,128]{1,0:T(8,128)(2,1)S(1)}, bf16[4112,128]{1,0:T(8,128)(2,1)}, u32[]{:S(2)}, u32[]{:S(2)}) %collective-permute-start) | collective-permute-done | bytes 1052704 | tf_op jit(solution)/shard_map/ppermute | solution.py:20
  31.0 0.7 slice_bitcast_fusion.5
  31.6 0.2 dynamic-update-slice
  31.8 9.3 %collective-permute-done.1.refs_4_.refs_9_ = bf16[4112,128]{1,0:T(8,128)(2,1)} collective-permute-done((bf16[4112,128]{1,0:T(8,128)(2,1)S(1)}, bf16[4112,128]{1,0:T(8,128)(2,1)}, u32[]{:S(2)}, u32[]{:S(2)}) %collective-permute-start.1) | collective-permute-done | bytes 1052704 | tf_op jit(solution)/shard_map/ppermute | solution.py:20
  41.1 0.7 slice_bitcast_fusion.4
  41.7 0.2 dynamic-update-slice.1
  41.9 35.1 %collective-permute-done.2.refs_5_.refs_10_ = bf16[4112,128]{1,0:T(8,128)(2,1)} collective-permute-done((bf16[4112,128]{1,0:T(8,128)(2,1)S(1)}, bf16[4112,128]{1,0:T(8,128)(2,1)}, u32[]{:S(2)}, u32[]{:S(2)}) %collective-permute-start.2) | collective-permute-done | bytes 1052704 | tf_op jit(solution)/shard_map/ppermute | solution.py:20
  77.0 0.7 slice_bitcast_fusion.3
  77.7 0.2 dynamic-update-slice.2
  77.8 0.0 collective-permute-done.3.refs_6_.refs_11_
  77.9 0.7 slice_bitcast_fusion.2
  78.5 0.2 dynamic-update-slice.3
  78.7 0.0 copy-start
  78.7 1.6 fusion.4.refs_2_
  80.4 0.0 copy-done
  80.4 32.0 %attention.1 = (bf16[256,2048]{1,0:T(8,128)(2,1)S(1)}, bf16[16,256,128]{2,1,0:T(8,128)(2,1)S(1)}, bf16[2,8,256,128]{3,2,1,0:T(8,128)(2,1)S(1)}, bf16[2,8,256,128...) custom-call(bf16[16,256,128]{2,1,0:T(8,128)(2,1)S(1)} %copy-done, ...), custom_call_target="tpu_custom_call" | custom-call | flops 6710886400 | bytes 12582912 | tf_op jit(solution)/shard_map/attention/pallas_call | solution.py:82
  112.4 0.0 copy-start.5
  112.4 0.0 copy-start.6
  112.4 0.0 copy-start.1
  112.4 0.0 copy-start.3
  112.4 0.1 copy.54
  112.5 0.9 copy-done.5
  113.4 0.3 copy-done.6
  113.7 39.7 %all_to_all.15 = bf16[16,2,8,2048]{3,2,1,0:T(8,128)(2,1)} all-to-all(bf16[16,2,8,2048]{3,2,1,0:T(8,128)(2,1)S(1)} %bitcast.44), channel_id=1, replica_groups=mesh['seq'=16,'head'=2] {'seq'}, dimensions={0} | all-to-all | bytes 2097152 | tf_op jit(solution)/shard_map/all_to_all | solution.py:161
  153.4 0.0 copy-done.1
  153.4 0.0 copy-done.3
  153.4 2.3 pick.1
  155.7 5.1 %all-to-all-start.1 = ((bf16[16,2,8,2048]{3,2,1,0:T(8,128)(2,1)}), bf16[16,2,8,2048]{3,2,1,0:T(8,128)(2,1)}, u32[]{:S(2)}, u32[]{:S(2)}) async-start(bf16[16,2,8,2048]{3,2,1,0:T(8,128)(2,1)} %bitcast.40), calls=%async_computation.1 | async-start | bytes 2097152 | tf_op jit(solution)/shard_map/all_to_all | solution.py:163
  160.8 3.1 %collective-permute-start.4 = (bf16[2,8,256,128]{3,2,1,0:T(8,128)(2,1)}, bf16[2,8,256,128]{3,2,1,0:T(8,128)(2,1)}, u32[]{:S(2)}, u32[]{:S(2)}) collective-permute-start(bf16[2,8,256,128]{3,2,1,0:T(8,128)(2,1)} %copy-done.6), channel_id=1, source_target_pairs={{2,0},{4,2},{6,4},{8,6},{10,8},{12,10},{14,12},{16,14},{18,16},{20... | collective-permute-start | bytes 3145736 | tf_op jit(solution)/shard_map/ppermute | solution.py:20
  163.9 2.3 collective-permute-start.5
  166.2 0.0 copy-done.4
  166.2 1.9 collective-permute-start.6
  168.1 0.0 copy-done.2
  168.1 1.9 collective-permute-start.7
  170.0 1.6 copy.46
  171.7 13.5 %all-to-all-done.1 = bf16[16,2,8,2048]{3,2,1,0:T(8,128)(2,1)} async-done(((bf16[16,2,8,2048]{3,2,1,0:T(8,128)(2,1)}), bf16[16,2,8,2048]{3,2,1,0:T(8,128)(2,1)}, u32[]{:S(2)}, u32[]{:S(2)}) %all-to-all-start.1) | async-done | bytes 1048608 | tf_op jit(solution)/shard_map/all_to_all | solution.py:163
  185.2 2.3 copy.53
  187.5 3.6 %all-to-all-start.2 = ((bf16[2,128,2048]{2,1,0:T(8,128)(2,1)}), bf16[2,128,2048]{2,1,0:T(8,128)(2,1)S(1)}, u32[]{:S(2)}, u32[]{:S(2)}) async-start(bf16[2,128,2048]{2,1,0:T(8,128)(2,1)} %bitcast.43), calls=%async_computation.2 | async-start | bytes 2097152 | tf_op jit(solution)/shard_map/all_to_all | solution.py:171
  191.1 10.3 %collective-permute-done.4 = bf16[2,8,256,128]{3,2,1,0:T(8,128)(2,1)} collective-permute-done((bf16[2,8,256,128]{3,2,1,0:T(8,128)(2,1)}, bf16[2,8,256,128]{3,2,1,0:T(8,128)(2,1)}, u32[]{:S(2)}, u32[]{:S(2)}) %collective-permute-start.4) | collective-permute-done | bytes 1048608 | tf_op jit(solution)/shard_map/ppermute | solution.py:20
  201.4 22.5 %collective-permute-done.5 = bf16[2,8,256,128]{3,2,1,0:T(8,128)(2,1)} collective-permute-done((bf16[2,8,256,128]{3,2,1,0:T(8,128)(2,1)}, bf16[2,8,256,128]{3,2,1,0:T(8,128)(2,1)}, u32[]{:S(2)}, u32[]{:S(2)}) %collective-permute-start.5) | collective-permute-done | bytes 1048608 | tf_op jit(solution)/shard_map/ppermute | solution.py:20
  223.9 21.9 %collective-permute-done.6 = bf16[2,8,256,128]{3,2,1,0:T(8,128)(2,1)} collective-permute-done((bf16[2,8,256,128]{3,2,1,0:T(8,128)(2,1)S(1)}, bf16[2,8,256,128]{3,2,1,0:T(8,128)(2,1)}, u32[]{:S(2)}, u32[]{:S(2)}) %collective-permute-start.6) | collective-permute-done | bytes 1048608 | tf_op jit(solution)/shard_map/ppermute | solution.py:20
  245.8 19.0 %collective-permute-done.7 = bf16[2,8,256,128]{3,2,1,0:T(8,128)(2,1)} collective-permute-done((bf16[2,8,256,128]{3,2,1,0:T(8,128)(2,1)S(1)}, bf16[2,8,256,128]{3,2,1,0:T(8,128)(2,1)}, u32[]{:S(2)}, u32[]{:S(2)}) %collective-permute-start.7) | collective-permute-done | bytes 1048608 | tf_op jit(solution)/shard_map/ppermute | solution.py:20
  264.7 3.5 %fusion.6 = bf16[2,256,8,128]{3,1,2,0:T(8,128)(2,1)S(1)} fusion(bf16[2,8,256,128]{3,2,1,0:T(8,128)(2,1)} %collective-permute-done.7, bf16[2,8,256,128]{3,2,1,0:T(8,128)(2,1)} %collective-permute-done.6, bf16[2,8,256,128]{3,2,1,0:T(8,128)(2,1)} %collective-permute-done.5, f32[2,8,256,128]{3,2,1,0:T(8,128)} %get-tuple-element.13, ...), kind=kLoop, calls=%fused_computation.10 | loop fusion | flops 4718592 | bytes 7340032 | tf_op jit(solution)/shard_map/convert_element_type | solution.py:177
  268.3 0.1 slice_bitcast_fusion
  268.4 1.1 copy.48
  269.5 1.1 copy.47
  270.7 0.0 all-to-all-done.2
  270.7 0.7 copy.44
  271.3 1.3 copy.45
  (8 shorter events, 0.0 us)
Async XLA Ops:
  0.6 1.9 copy-start.8
  2.6 12.7 %copy-start.9 = (s32[256]{0:T(256)S(1)}, s32[256]{0:T(256)}, u32[]{:S(2)}) copy-start(s32[256]{0:T(256)} %param.10) | copy-start | bytes 3076
  2.6 12.7 %copy-start.7 = (bf16[256,16,128]{2,1,0:T(8,128)(2,1)S(1)}, bf16[256,16,128]{2,1,0:T(8,128)(2,1)}, u32[]{:S(2)}) copy-start(bf16[256,16,128]{2,1,0:T(8,128)(2,1)} %param.9) | copy-start | bytes 3145732
  2.7 28.3 %collective-permute-start = (bf16[4112,128]{1,0:T(8,128)(2,1)S(1)}, bf16[4112,128]{1,0:T(8,128)(2,1)}, u32[]{:S(2)}, u32[]{:S(2)}) collective-permute-start(bf16[4112,128]{1,0:T(8,128)(2,1)S(1)} %fusion.5.refs_7_.refs_12_), channel_id=1, source_target_pairs={{0,8},{2,10},{4,12},{6,14},{8,16},{10,18},{12,20},{14,22},{16,24},... | collective-permute-start | bytes 3158024 | tf_op jit(solution)/shard_map/ppermute | solution.py:20
  6.3 34.8 %collective-permute-start.1 = (bf16[4112,128]{1,0:T(8,128)(2,1)S(1)}, bf16[4112,128]{1,0:T(8,128)(2,1)}, u32[]{:S(2)}, u32[]{:S(2)}) collective-permute-start(bf16[4112,128]{1,0:T(8,128)(2,1)S(1)} %fusion.5.refs_7_.refs_12_), channel_id=1, source_target_pairs={{0,6},{2,8},{4,10},{6,12},{8,14},{10,16},{12,18},{14,20},{16,22},{... | collective-permute-start | bytes 3158024 | tf_op jit(solution)/shard_map/ppermute | solution.py:20
  8.9 69.0 %collective-permute-start.3 = (bf16[4112,128]{1,0:T(8,128)(2,1)S(1)}, bf16[4112,128]{1,0:T(8,128)(2,1)}, u32[]{:S(2)}, u32[]{:S(2)}) collective-permute-start(bf16[4112,128]{1,0:T(8,128)(2,1)S(1)} %fusion.5.refs_7_.refs_12_), channel_id=1, source_target_pairs={{0,2},{2,4},{4,6},{6,8},{8,10},{10,12},{12,14},{14,16},{16,18},{18... | collective-permute-start | bytes 3158024 | tf_op jit(solution)/shard_map/ppermute | solution.py:20
  11.8 65.2 %collective-permute-start.2 = (bf16[4112,128]{1,0:T(8,128)(2,1)S(1)}, bf16[4112,128]{1,0:T(8,128)(2,1)}, u32[]{:S(2)}, u32[]{:S(2)}) collective-permute-start(bf16[4112,128]{1,0:T(8,128)(2,1)S(1)} %fusion.5.refs_7_.refs_12_), channel_id=1, source_target_pairs={{0,4},{2,6},{4,8},{6,10},{8,12},{10,14},{12,16},{14,18},{16,20},{1... | collective-permute-start | bytes 3158024 | tf_op jit(solution)/shard_map/ppermute | solution.py:20
  78.7 1.7 copy-start
  112.4 1.0 copy-start.5
  112.4 1.3 copy-start.6
  112.4 41.0 %copy-start.1 = (bf16[2,8,256,128]{3,2,1,0:T(8,128)(2,1)}, bf16[2,8,256,128]{3,2,1,0:T(8,128)(2,1)S(1)}, u32[]{:S(2)}) copy-start(bf16[2,8,256,128]{3,2,1,0:T(8,128)(2,1)S(1)} %get-tuple-element.17) | copy-start | bytes 3145732
  112.4 41.0 %copy-start.3 = (bf16[2,8,256,128]{3,2,1,0:T(8,128)(2,1)}, bf16[2,8,256,128]{3,2,1,0:T(8,128)(2,1)S(1)}, u32[]{:S(2)}) copy-start(bf16[2,8,256,128]{3,2,1,0:T(8,128)(2,1)S(1)} %get-tuple-element.16) | copy-start | bytes 3145732
  155.7 10.5 %copy-start.4 = (bf16[2,8,256,128]{3,2,1,0:T(8,128)(2,1)S(1)}, bf16[2,8,256,128]{3,2,1,0:T(8,128)(2,1)}, u32[]{:S(2)}) copy-start(bf16[2,8,256,128]{3,2,1,0:T(8,128)(2,1)} %copy-done.3) | copy-start | bytes 3145732
  155.7 12.4 %copy-start.2 = (bf16[2,8,256,128]{3,2,1,0:T(8,128)(2,1)S(1)}, bf16[2,8,256,128]{3,2,1,0:T(8,128)(2,1)}, u32[]{:S(2)}) copy-start(bf16[2,8,256,128]{3,2,1,0:T(8,128)(2,1)} %copy-done.1) | copy-start | bytes 3145732
  155.7 29.6 %all-to-all-start.1 = ((bf16[16,2,8,2048]{3,2,1,0:T(8,128)(2,1)}), bf16[16,2,8,2048]{3,2,1,0:T(8,128)(2,1)}, u32[]{:S(2)}, u32[]{:S(2)}) async-start(bf16[16,2,8,2048]{3,2,1,0:T(8,128)(2,1)} %bitcast.40), calls=%async_computation.1 | async-start | bytes 2097152 | tf_op jit(solution)/shard_map/all_to_all | solution.py:163
  160.8 40.6 %collective-permute-start.4 = (bf16[2,8,256,128]{3,2,1,0:T(8,128)(2,1)}, bf16[2,8,256,128]{3,2,1,0:T(8,128)(2,1)}, u32[]{:S(2)}, u32[]{:S(2)}) collective-permute-start(bf16[2,8,256,128]{3,2,1,0:T(8,128)(2,1)} %copy-done.6), channel_id=1, source_target_pairs={{2,0},{4,2},{6,4},{8,6},{10,8},{12,10},{14,12},{16,14},{18,16},{20... | collective-permute-start | bytes 3145736 | tf_op jit(solution)/shard_map/ppermute | solution.py:20
  163.9 60.0 %collective-permute-start.5 = (bf16[2,8,256,128]{3,2,1,0:T(8,128)(2,1)}, bf16[2,8,256,128]{3,2,1,0:T(8,128)(2,1)}, u32[]{:S(2)}, u32[]{:S(2)}) collective-permute-start(bf16[2,8,256,128]{3,2,1,0:T(8,128)(2,1)} %copy-done.5), channel_id=1, source_target_pairs={{4,0},{6,2},{8,4},{10,6},{12,8},{14,10},{16,12},{18,14},{20,16},{2... | collective-permute-start | bytes 3145736 | tf_op jit(solution)/shard_map/ppermute | solution.py:20
  166.2 79.6 %collective-permute-start.6 = (bf16[2,8,256,128]{3,2,1,0:T(8,128)(2,1)S(1)}, bf16[2,8,256,128]{3,2,1,0:T(8,128)(2,1)}, u32[]{:S(2)}, u32[]{:S(2)}) collective-permute-start(bf16[2,8,256,128]{3,2,1,0:T(8,128)(2,1)S(1)} %copy-done.4), channel_id=1, source_target_pairs={{6,0},{8,2},{10,4},{12,6},{14,8},{16,10},{18,12},{20,14},{22,16},{... | collective-permute-start | bytes 3145736 | tf_op jit(solution)/shard_map/ppermute | solution.py:20
  168.1 96.6 %collective-permute-start.7 = (bf16[2,8,256,128]{3,2,1,0:T(8,128)(2,1)S(1)}, bf16[2,8,256,128]{3,2,1,0:T(8,128)(2,1)}, u32[]{:S(2)}, u32[]{:S(2)}) collective-permute-start(bf16[2,8,256,128]{3,2,1,0:T(8,128)(2,1)S(1)} %copy-done.2), channel_id=1, source_target_pairs={{8,0},{10,2},{12,4},{14,6},{16,8},{18,10},{20,12},{22,14},{24,16},... | collective-permute-start | bytes 3145736 | tf_op jit(solution)/shard_map/ppermute | solution.py:20
  187.5 83.1 %all-to-all-start.2 = ((bf16[2,128,2048]{2,1,0:T(8,128)(2,1)}), bf16[2,128,2048]{2,1,0:T(8,128)(2,1)S(1)}, u32[]{:S(2)}, u32[]{:S(2)}) async-start(bf16[2,128,2048]{2,1,0:T(8,128)(2,1)} %bitcast.43), calls=%async_computation.2 | async-start | bytes 2097152 | tf_op jit(solution)/shard_map/all_to_all | solution.py:171

commit v2 on v1

v2 whole, which is shorter than its diff:
```python
import functools

import jax
import jax.numpy as jnp
from jax import lax
from jax.experimental import pallas as pl
from jax.experimental.pallas import tpu as pltpu
from jax.sharding import PartitionSpec as P

WINDOW_LENGTH = 1024
QSCALAR = 168
FACTOR = QSCALAR ** (-0.5)
LOG2E = 1.4426950408889634
SEG_ROWS = 16
MESH = pl.DeviceIdType.MESH


def dot(a, b, ca, cb):
    return lax.dot_general(a, b, (((ca,), (cb,)), ((), ())), preferred_element_type=jnp.float32)


def attention_kernel(
    n_seq,
    q_ref,
    do_ref,
    seg_ref,
    own_ref,
    o_ref,
    dq_ref,
    g_ref,
    kv_in,
    p_scr,
    bias,
    g_x,
    g_z,
    g_own,
    g_out,
    g_in,
    send,
    recv,
    g_send,
    g_recv,
):
    heads, rows_kv, dim = own_ref.shape
    tok = seg_ref.shape[0]
    width = q_ref.shape[0] // heads
    rows = width * tok
    me = lax.axis_index("seq")
    core = lax.rem(me, 2)
    half = lax.rem(me // 2, 2)
    plane = me // 4
    planes = n_seq // 4
    core_peer = me + 1 - 2 * core
    x_peer = me + 2 - 4 * half
    has_prev = plane > 0
    has_next = plane < planes - 1
    Z, X, C, D = 0, 1, 2, 3

    barrier = pltpu.get_barrier_semaphore()

    def greet(who):
        pl.semaphore_signal(barrier, inc=1, device_id={"seq": who}, device_id_type=MESH)

    greet(core_peer)
    greet(x_peer)

    @pl.when(has_prev)
    def _():
        greet(me - 4)

    @pl.when(has_next)
    def _():
        greet(me + 4)

    pl.semaphore_wait(barrier, 2 + has_prev.astype(jnp.int32) + has_next.astype(jnp.int32))

    def copy(kind, h, src, who):
        return pltpu.make_async_remote_copy(
            src_ref=src,
            dst_ref=kv_in.at[kind, h],
            send_sem=send.at[kind, h],
            recv_sem=recv.at[kind, h],
            device_id={"seq": who},
            device_id_type=MESH,
        )

    def z_copy(h):
        return copy(Z, h, own_ref.at[h], me + 4)

    def x_copy(h, src):
        return copy(X, h, src.at[h], x_peer)

    def c_copy(h, src):
        return copy(C, h, src.at[h], core_peer)

    def d_copy(h):
        return copy(D, h, kv_in.at[X, h], core_peer)

    @pl.loop(0, heads)
    def _(h):
        @pl.when(has_next)
        def _():
            z_copy(h).start()

        @pl.when(half == 0)
        def _():
            x_copy(h, own_ref).start()

        @pl.when(core == 0)
        def _():
            c_copy(h, own_ref).start()

        @pl.when(jnp.logical_not(has_prev))
        def _():
            kv_in[Z, h] = jnp.zeros((rows_kv, dim), jnp.bfloat16)

    def stage_z(h):
        @pl.when(has_prev)
        def _():
            copy(Z, h, own_ref.at[h], me - 4).wait_recv()

        @pl.when(half == 1)
        def _():
            x_copy(h, kv_in.at[Z]).start()

        @pl.when(core == 1)
        def _():
            c_copy(h, kv_in.at[Z]).start()

    def stage_x(h):
        x_copy(h, own_ref).wait_recv()
        d_copy(h).start()

    def stage_c(h):
        c_copy(h, own_ref).wait_recv()
        d_copy(h).wait_recv()

    def gcopy(kind, h, who):
        return pltpu.make_async_remote_copy(
            src_ref=g_out.at[kind, h],
            dst_ref=g_in.at[kind, h],
            send_sem=g_send.at[kind, h],
            recv_sem=g_recv.at[kind, h],
            device_id={"seq": who},
            device_id_type=MESH,
        )

    def grad_x(h):
        gcopy(D, h, core_peer).wait_recv()
        total = g_x[h] + g_in[D, h].astype(jnp.float32)
        g_out[X, h] = total.astype(jnp.bfloat16)
        gcopy(X, h, x_peer).start()

    def grad_z(h):
        gcopy(C, h, core_peer).wait_recv()
        gcopy(X, h, x_peer).wait_recv()
        from_c = g_in[C, h].astype(jnp.float32)
        from_x = g_in[X, h].astype(jnp.float32)
        zero = jnp.zeros_like(from_c)
        back = g_z[h] + jnp.where(core == 1, from_c, zero) + jnp.where(half == 1, from_x, zero)
        g_out[Z, h] = back.astype(jnp.bfloat16)
        g_own[h] = g_own[h] + jnp.where(core == 0, from_c, zero) + jnp.where(half == 0, from_x, zero)

        @pl.when(has_prev)
        def _():
            gcopy(Z, h, me - 4).start()

    def finish(h):
        @pl.when(has_next)
        def _():
            gcopy(Z, h, me + 4).wait_recv()
            g_ref[h] = (g_own[h] + g_in[Z, h].astype(jnp.float32)).astype(jnp.bfloat16)

        @pl.when(jnp.logical_not(has_next))
        def _():
            g_ref[h] = g_own[h].astype(jnp.bfloat16)

    spans = (4, 2, 3 - 2 * core, 1 + 2 * core, 0)

    def chunk(b, h):
        return own_ref.at[h] if b == 4 else kv_in.at[b, h]

    def masks():
        gap = lax.broadcasted_iota(jnp.int32, (tok, tok), 0) - lax.broadcasted_iota(
            jnp.int32, (tok, tok), 1
        )
        seg_q = seg_ref[...]
        for b in range(5):
            segs = chunk(b, 0)[2 * tok :, :].astype(jnp.float32)
            seg_k = jnp.concatenate([segs[r : r + 1] for r in range(tok // dim)], axis=1)
            far = gap + spans[b] * tok
            near = jnp.where(me >= spans[b], WINDOW_LENGTH, -1)
            allowed = (far >= 0) & (far < near) & (seg_q == seg_k)
            bias[b] = jnp.where(allowed, 0.0, -jnp.inf)

    def compute(h):
        q = q_ref[pl.ds(h * width, width)].reshape(rows, dim)
        do = do_ref[pl.ds(h * width, width)].reshape(rows, dim)
        top = None
        for b in range(5):
            s = dot(q, chunk(b, h)[:tok, :], 1, 1).reshape(width, tok, tok)
            s = (s + bias[b][None]).reshape(rows, tok)
            p_scr[b] = s
            m = jnp.max(s, axis=1, keepdims=True)
            top = m if top is None else jnp.maximum(top, m)
        total = jnp.zeros((rows, 1), jnp.float32)
        for b in range(5):
            p = jnp.exp2((p_scr[b] - top) * (FACTOR * LOG2E))
            p_scr[b] = p
            total += jnp.sum(p, axis=1, keepdims=True)
        scale = 1.0 / total

        def put(b, part, value):
            at = pl.ds(part * tok, tok)
            if b == 4:
                g_own[h, at] = value
            elif b == Z:
                g_z[h, at] = value
            elif b == X:
                g_x[h, at] = value
            else:
                g_out[b, h, at] = value.astype(jnp.bfloat16)

        out = jnp.zeros((rows, dim), jnp.float32)
        for b in range(5):
            w = p_scr[b] * scale
            p_scr[b] = w
            probs = w.astype(jnp.bfloat16)
            out += dot(probs, chunk(b, h)[tok : 2 * tok, :], 1, 0)
            put(b, 1, dot(probs, do, 0, 0))
        out = out.astype(jnp.bfloat16)
        for w in range(width):
            at = pl.ds(pl.multiple_of((h * width + w) * dim, dim), dim)
            o_ref[:, at] = out[w * tok : (w + 1) * tok]
        delta = jnp.sum(do.astype(jnp.float32) * out.astype(jnp.float32), axis=1, keepdims=True)
        dq = jnp.zeros((rows, dim), jnp.float32)
        for b in range(5):
            dp = dot(do, chunk(b, h)[tok : 2 * tok, :], 1, 1)
            ds = (p_scr[b] * (dp - delta)).astype(jnp.bfloat16)
            dq += dot(ds, chunk(b, h)[:tok, :], 1, 0)
            put(b, 0, FACTOR * dot(ds, q, 0, 0))
        dq_ref[pl.ds(h * width, width)] = (FACTOR * dq).astype(jnp.bfloat16).reshape(width, tok, dim)

    stage_z(0)
    stage_z(1)
    stage_x(0)
    stage_c(0)
    masks()

    @pl.loop(0, heads)
    def _(h):
        @pl.when(h + 2 < heads)
        def _():
            stage_z(h + 2)

        @pl.when(h + 1 < heads)
        def _():
            stage_x(h + 1)

        @pl.when(h > 0)
        def _():
            stage_c(h)

        compute(h)
        gcopy(D, h, core_peer).start()
        gcopy(C, h, core_peer).start()

        @pl.when(h >= 1)
        def _():
            grad_x(h - 1)

        @pl.when(h >= 2)
        def _():
            grad_z(h - 2)

    grad_x(heads - 1)
    grad_z(heads - 2)
    grad_z(heads - 1)

    @pl.loop(0, heads)
    def _(h):
        finish(h)

        @pl.when(has_next)
        def _():
            z_copy(h).wait_send()

        x_copy(h, own_ref).wait_send()
        c_copy(h, own_ref).wait_send()
        d_copy(h).wait_send()
        gcopy(D, h, core_peer).wait_send()
        gcopy(C, h, core_peer).wait_send()
        gcopy(X, h, x_peer).wait_send()

        @pl.when(has_prev)
        def _():
            gcopy(Z, h, me - 4).wait_send()


def attention(q, do, seg, own):
    heads, tok, dim = q.shape
    kv_heads, rows_kv, _ = own.shape
    width = heads // kv_heads
    pairs = heads * tok * tok * 5
    vmem = pl.BlockSpec(memory_space=pltpu.VMEM)
    grad = (kv_heads, 2 * tok, dim)
    return pl.pallas_call(
        functools.partial(attention_kernel, lax.axis_size("seq")),
        in_specs=[vmem] * 4,
        out_specs=[vmem] * 3,
        out_shape=[
            jax.ShapeDtypeStruct((tok, heads * dim), jnp.bfloat16),
            jax.ShapeDtypeStruct((heads, tok, dim), jnp.bfloat16),
            jax.ShapeDtypeStruct(grad, jnp.bfloat16),
        ],
        scratch_shapes=[
            pltpu.VMEM((4,) + own.shape, jnp.bfloat16),
            pltpu.VMEM((5, width * tok, tok), jnp.float32),
            pltpu.VMEM((5, tok, tok), jnp.float32),
            pltpu.VMEM(grad, jnp.float32),
            pltpu.VMEM(grad, jnp.float32),
            pltpu.VMEM(grad, jnp.float32),
            pltpu.VMEM((4,) + grad, jnp.bfloat16),
            pltpu.VMEM((4,) + grad, jnp.bfloat16),
            pltpu.SemaphoreType.DMA((4, kv_heads)),
            pltpu.SemaphoreType.DMA((4, kv_heads)),
            pltpu.SemaphoreType.DMA((4, kv_heads)),
            pltpu.SemaphoreType.DMA((4, kv_heads)),
        ],
        compiler_params=pltpu.CompilerParams(
            vmem_limit_bytes=48 * 2**20, collective_id=0, has_side_effects=True
        ),
        cost_estimate=pl.CostEstimate(
            flops=10 * pairs * dim, bytes_accessed=8 * 2**20, transcendentals=pairs
        ),
        name="attention",
    )(q, do, seg, own)


def pick_kernel(order_ref, held_ref, out_ref):
    for q in range(out_ref.shape[0]):
        out_ref[q] = held_ref[order_ref[q]]


def pick(held, order):
    return pl.pallas_call(
        pick_kernel,
        in_specs=[
            pl.BlockSpec(memory_space=pltpu.SMEM),
            pl.BlockSpec(memory_space=pltpu.VMEM),
        ],
        out_specs=pl.BlockSpec(memory_space=pltpu.VMEM),
        out_shape=jax.ShapeDtypeStruct(held.shape, held.dtype),
        name="pick",
    )(order, held)


def local(queries, keys, values, output_gradient, segment_ids, block_order):
    tok, q_heads, dim = queries.shape
    kv_heads = keys.shape[1]
    seq_count = lax.axis_size("seq")
    head_count = lax.axis_size("head")
    seg = segment_ids.astype(jnp.float32)
    seg_rows = seg.astype(jnp.bfloat16).reshape(tok // dim, dim)
    seg_rows = jnp.pad(seg_rows, ((0, SEG_ROWS - tok // dim), (0, 0)))
    own = jnp.concatenate(
        [
            jnp.moveaxis(keys, 1, 0),
            jnp.moveaxis(values, 1, 0),
            jnp.broadcast_to(seg_rows[None], (kv_heads, SEG_ROWS, dim)),
        ],
        axis=1,
    )
    attended, dq, grads = attention(
        jnp.moveaxis(queries, 1, 0), jnp.moveaxis(output_gradient, 1, 0), seg[:, None], own
    )

    nb = block_order.shape[0] // seq_count
    piece = tok // nb // seq_count
    features = q_heads * dim
    flat = jnp.swapaxes(attended.reshape(nb, seq_count, piece, features), 0, 1)
    spread = lax.all_to_all(flat, "seq", split_axis=0, concat_axis=0, tiled=True)
    ordered = pick(spread.reshape(nb * seq_count, piece, features), block_order)
    delivered = lax.all_to_all(
        ordered.reshape(seq_count, nb, piece, features),
        "seq",
        split_axis=0,
        concat_axis=0,
        tiled=True,
    )
    reordered = jnp.swapaxes(delivered, 0, 1).reshape(head_count, tok // head_count, features)
    halves = lax.all_to_all(reordered, "head", split_axis=0, concat_axis=0, tiled=True)
    relaid = jnp.swapaxes(halves, 0, 1).reshape(tok // head_count, head_count * features)

    grads = jnp.moveaxis(grads.reshape(kv_heads, 2, tok, dim), 0, 2)
    return (relaid, jnp.moveaxis(dq, 0, 1), grads[0], grads[1])


def solution(mesh):
    placed = (
        P("seq", "head", None),
        P("seq", "head", None),
        P("seq", "head", None),
        P("seq", "head", None),
        P("seq"),
        P(),
    )
    return jax.shard_map(
        local,
        mesh=mesh,
        in_specs=placed,
        out_specs=(
            P(("seq", "head"), None),
            P("seq", "head", None),
            P("seq", "head", None),
            P("seq", "head", None),
        ),
        check_vma=False,
    )
```

time: 273 us -> 159 us (0.58)
  waiting for transfers between devices: 144 us -> 11.3 us
  Pallas kernels: 34.3 us -> 71.1 us
  starting transfers between devices: 30.4 us -> 3.58 us
  blocking collectives: 39.7 us -> 60.3 us
  local copies, waits for them, and re-layouts: 16.9 us -> 8.97 us
  other arithmetic: 6.03 us -> 1.74 us
    ppermute x8 -> x0, waiting for transfers between devices: 131 us -> none  [shifted(): return lax.ppermute(value, axis, pairs)]
    pallas_call x1, Pallas kernels: 32 us -> 68.8 us  [attention(): pl.pallas_call(functools.partial(attention_kernel, lax.axis_size('seq')),...]
    all_to_all x0 -> x1, blocking collectives: none -> 29.8 us  [local(): lax.all_to_all(ordered.reshape(seq_count, nb, piece, features), 'seq', sp...]
    ppermute x8 -> x0, starting transfers between devices: 21.8 us -> none  [shifted(): return lax.ppermute(value, axis, pairs)]
    all_to_all x1 -> x0, waiting for transfers between devices: 13.5 us -> none  [local(): lax.all_to_all(ordered.reshape(seq_count, nb, piece, features), 'seq', sp...]
    all_to_all x1, waiting for transfers between devices: 0.01 us -> 11.3 us  [local(): lax.all_to_all(reordered, 'head', split_axis=0, concat_axis=0, tiled=True)]
    all_to_all x1, blocking collectives: 39.7 us -> 30.5 us  [local(): lax.all_to_all(flat, 'seq', split_axis=0, concat_axis=0, tiled=True)]
    all_to_all x1 -> x0, starting transfers between devices: 5.09 us -> none  [local(): lax.all_to_all(ordered.reshape(seq_count, nb, piece, features), 'seq', sp...]
  transfers between devices with their start and end apart: 10 -> 1, of which waited for: 8 -> 1; matrix products, arithmetic and copies ran while one was open for 6% -> 2% of each run, Pallas kernels for 0% -> 0%
where the time goes in v2:
time: 159 us; the launch traced here: 158 us
  Pallas kernels  71.1 us (45%)
  blocking collectives  60.3 us (38%)
  waiting for transfers between devices  11.3 us (7%)
  local copies, waits for them, and re-layouts  8.97 us (6%)
  starting transfers between devices  3.58 us (2%)
  other arithmetic  1.74 us (1%)
    pallas_call x1, Pallas kernels, attention(): pl.pallas_call(functools.partial(attention_kernel, lax.axis_size('seq')),...  68.8 us
    all_to_all x1, blocking collectives, local(): lax.all_to_all(flat, 'seq', split_axis=0, concat_axis=0, tiled=True)  30.5 us
    all_to_all x1, blocking collectives, local(): lax.all_to_all(ordered.reshape(seq_count, nb, piece, features), 'seq', sp...  29.8 us
    all_to_all x1, waiting for transfers between devices, local(): lax.all_to_all(reordered, 'head', split_axis=0, concat_axis=0, tiled=True)  11.3 us
    all_to_all x1, starting transfers between devices, local(): lax.all_to_all(reordered, 'head', split_axis=0, concat_axis=0, tiled=True)  3.58 us
    unnamed x6, local copies, waits for them, and re-layouts  3.25 us
  transfers between devices with their start and end apart: 1, of which 1 were waited for; matrix products, arithmetic and copies ran while one was open for 2% of the time, Pallas kernels for 0%

profile of v2, /device:TPU:8, one launch (start us, length us, event | category | flops | bytes accessed | tf_op | source)
XLA Modules:
  0.0 157.7 jit_solution(7643228992377974737)
XLA Ops:
  0.6 0.7 convert_bitcast_fusion
  1.3 0.1 copy.41.seg_ref
  1.5 0.0 copy-start
  1.5 0.0 copy-start.1
  1.5 1.5 copy_bitcast_fusion.5
  3.0 0.0 copy-done
  3.0 0.3 copy-done.1
  3.3 0.5 copy_bitcast_fusion.3
  3.9 1.1 pad_maximum_fusion.own_ref
  4.9 68.8 %attention.1 = (bf16[256,2048]{1,0:T(8,128)(2,1)S(1)}, bf16[16,256,128]{2,1,0:T(8,128)(2,1)S(1)}, bf16[8,512,128]{2,1,0:T(8,128)(2,1)S(1)}) custom-call(bf16[16,256,128]{2,1,0:T(8,128)(2,1)S(1)} %get-tuple-element.33.q_ref, bf16[16,256,128]{2,1,0:T(8,128)(2,1)S(1)} %get-tuple-element.32.do_ref, f32[256,1]{1,0:T(8,128)S(1)} %copy.41.seg_ref, ...), custom_call_target="tpu_custom_call" | custom-call | flops 6710886400 | bytes 8388608 | tf_op jit(solution)/shard_map/attention/pallas_call | solution.py:307
  73.7 0.1 copy.57
  73.8 30.5 %all_to_all.15 = bf16[16,2,8,2048]{3,2,1,0:T(8,128)(2,1)} all-to-all(bf16[16,2,8,2048]{3,2,1,0:T(8,128)(2,1)S(1)} %bitcast.41), channel_id=1, replica_groups=mesh['seq'=16,'head'=2] {'seq'}, dimensions={0} | all-to-all | bytes 2097152 | tf_op jit(solution)/shard_map/all_to_all | solution.py:382
  104.3 2.3 %pick.1 = bf16[32,8,2048]{2,1,0:T(8,128)(2,1)} custom-call(s32[32]{0:T(128)} %order_ref.1, bf16[32,8,2048]{2,1,0:T(8,128)(2,1)} %bitcast.36), custom_call_target="tpu_custom_call" | custom-call | tf_op jit(solution)/shard_map/pick/pallas_call | solution.py:346
  106.6 29.8 %all_to_all.16 = bf16[16,2,8,2048]{3,2,1,0:T(8,128)(2,1)S(1)} all-to-all(bf16[16,2,8,2048]{3,2,1,0:T(8,128)(2,1)} %bitcast.37), channel_id=1, replica_groups=mesh['seq'=16,'head'=2] {'seq'}, dimensions={0} | all-to-all | bytes 2097152 | tf_op jit(solution)/shard_map/all_to_all | solution.py:384
  136.4 1.0 copy.56
  137.5 3.6 %all-to-all-start.2 = ((bf16[2,128,2048]{2,1,0:T(8,128)(2,1)}), bf16[2,128,2048]{2,1,0:T(8,128)(2,1)S(1)}, u32[]{:S(2)}, u32[]{:S(2)}) async-start(bf16[2,128,2048]{2,1,0:T(8,128)(2,1)} %bitcast.39), calls=%async_computation.2 | async-start | bytes 2097152 | tf_op jit(solution)/shard_map/all_to_all | solution.py:392
  141.0 1.6 %copy.47 = bf16[256,16,128]{2,1,0:T(8,128)(2,1)} copy(bf16[256,16,128]{2,0,1:T(8,128)(2,1)S(1)} %bitcast.34) | data formatting | bytes 2097152
  142.7 0.7 copy.55
  143.4 1.0 slice_bitcast_fusion
  144.4 11.3 %all-to-all-done.2 = bf16[2,128,2048]{2,1,0:T(8,128)(2,1)S(1)} async-done(((bf16[2,128,2048]{2,1,0:T(8,128)(2,1)}), bf16[2,128,2048]{2,1,0:T(8,128)(2,1)S(1)}, u32[]{:S(2)}, u32[]{:S(2)}) %all-to-all-start.2) | async-done | bytes 1048608 | tf_op jit(solution)/shard_map/all_to_all | solution.py:392
  155.7 0.7 copy.44
  156.4 1.3 copy.46
  (2 shorter events, 0.0 us)
Async XLA Ops:
  1.5 1.6 %copy-start = (bf16[256,16,128]{2,1,0:T(8,128)(2,1)S(1)}, bf16[256,16,128]{2,1,0:T(8,128)(2,1)}, u32[]{:S(2)}) copy-start(bf16[256,16,128]{2,1,0:T(8,128)(2,1)} %param.9) | copy-start | bytes 3145732
  1.5 1.9 %copy-start.1 = (bf16[256,16,128]{2,1,0:T(8,128)(2,1)S(1)}, bf16[256,16,128]{2,1,0:T(8,128)(2,1)}, u32[]{:S(2)}) copy-start(bf16[256,16,128]{2,1,0:T(8,128)(2,1)} %param.6) | copy-start | bytes 3145732
  137.5 18.3 %all-to-all-start.2 = ((bf16[2,128,2048]{2,1,0:T(8,128)(2,1)}), bf16[2,128,2048]{2,1,0:T(8,128)(2,1)S(1)}, u32[]{:S(2)}, u32[]{:S(2)}) async-start(bf16[2,128,2048]{2,1,0:T(8,128)(2,1)} %bitcast.39), calls=%async_computation.2 | async-start | bytes 2097152 | tf_op jit(solution)/shard_map/all_to_all | solution.py:392

commit v3 on v2

--- a/solution.py
+++ b/solution.py
@@ -21,10 +21,13 @@
 
 def attention_kernel(
     n_seq,
+    n_head,
+    relay,
     q_ref,
     do_ref,
     seg_ref,
     own_ref,
+    order_ref,
     o_ref,
     dq_ref,
     g_ref,
@@ -40,6 +43,13 @@
     recv,
     g_send,
     g_recv,
+    o_out=None,
+    held=None,
+    picked=None,
+    o_send=None,
+    o_recv=None,
+    r_send=None,
+    r_recv=None,
 ):
     heads, rows_kv, dim = own_ref.shape
     tok = seg_ref.shape[0]
@@ -57,22 +67,39 @@
     Z, X, C, D = 0, 1, 2, 3
 
     barrier = pltpu.get_barrier_semaphore()
-
-    def greet(who):
-        pl.semaphore_signal(barrier, inc=1, device_id={"seq": who}, device_id_type=MESH)
-
-    greet(core_peer)
-    greet(x_peer)
-
-    @pl.when(has_prev)
-    def _():
-        greet(me - 4)
-
-    @pl.when(has_next)
-    def _():
-        greet(me + 4)
-
-    pl.semaphore_wait(barrier, 2 + has_prev.astype(jnp.int32) + has_next.astype(jnp.int32))
+    side = lax.axis_index("head")
+    slot = me * n_head + side
+    n_dev = n_seq * n_head
+
+    def greet(who, which):
+        pl.semaphore_signal(
+            barrier, inc=1, device_id={"seq": who, "head": which}, device_id_type=MESH
+        )
+
+    if relay:
+
+        @pl.loop(1, n_dev)
+        def _(k):
+            other = lax.rem(slot + k, n_dev)
+            greet(other // n_head, lax.rem(other, n_head))
+
+        pl.semaphore_wait(barrier, n_dev - 1)
+    else:
+        greet(core_peer, side)
+        greet(x_peer, side)
+
+        @pl.when(has_prev)
+        def _():
+            greet(me - 4, side)
+
+        @pl.when(has_next)
+        def _():
+            greet(me + 4, side)
+
+        pl.semaphore_wait(barrier, 2 + has_prev.astype(jnp.int32) + has_next.astype(jnp.int32))
+
+    def turn(step, at):
+        return lax.rem(step + 2 * at, heads)
 
     def copy(kind, h, src, who):
         return pltpu.make_async_remote_copy(
@@ -97,10 +124,12 @@
         return copy(D, h, kv_in.at[X, h], core_peer)
 
     @pl.loop(0, heads)
-    def _(h):
+    def _(step):
+        h = turn(step, plane)
+
         @pl.when(has_next)
         def _():
-            z_copy(h).start()
+            z_copy(turn(step, plane + 1)).start()
 
         @pl.when(half == 0)
         def _():
@@ -186,12 +215,75 @@
         )
         seg_q = seg_ref[...]
         for b in range(5):
-            segs = chunk(b, 0)[2 * tok :, :].astype(jnp.float32)
+            segs = chunk(b, turn(0, plane))[2 * tok :, :].astype(jnp.float32)
             seg_k = jnp.concatenate([segs[r : r + 1] for r in range(tok // dim)], axis=1)
             far = gap + spans[b] * tok
             near = jnp.where(me >= spans[b], WINDOW_LENGTH, -1)
             allowed = (far >= 0) & (far < near) & (seg_q == seg_k)
             bias[b] = jnp.where(allowed, 0.0, -jnp.inf)
+
+    def ocopy(head, source):
+        return pltpu.make_async_remote_copy(
+            src_ref=o_out.at[head],
+            dst_ref=held.at[source],
+            send_sem=o_send.at[head],
+            recv_sem=o_recv.at[source],
+            device_id={"seq": head},
+            device_id_type=MESH,
+        )
+
+    def send_out(head, part):
+        part = part.reshape(o_out.shape[1:])
+
+        @pl.when(head == me)
+        def _():
+            held[me] = part
+
+        @pl.when(head != me)
+        def _():
+            o_out[head] = part
+            ocopy(head, me).start()
+
+    def rcopy(block, source):
+        column = lax.rem(source, n_head) * n_seq + source // n_head
+        return pltpu.make_async_remote_copy(
+            src_ref=picked.at[block],
+            dst_ref=o_ref.at[:, pl.ds(pl.multiple_of(column * dim, dim), dim)],
+            send_sem=r_send.at[block],
+            recv_sem=r_recv.at[source],
+            device_id={"seq": block // n_head, "head": lax.rem(block, n_head)},
+            device_id_type=MESH,
+        )
+
+    def pick_and_send():
+        @pl.loop(1, n_seq)
+        def _(k):
+            other = lax.rem(me + k, n_seq)
+            ocopy(other, other).wait_recv()
+
+        per = n_dev // n_seq
+
+        @pl.loop(1, n_dev)
+        def _(k):
+            block = lax.rem(slot + k, n_dev)
+            source = order_ref[block]
+            picked[block] = held[source // per, lax.rem(source, per)]
+            rcopy(block, slot).start()
+
+        source = order_ref[slot]
+        column = (side * n_seq + me) * dim
+        o_ref[:, pl.ds(pl.multiple_of(column, dim), dim)] = held[source // per, lax.rem(source, per)]
+
+    def settle():
+        @pl.loop(1, n_seq)
+        def _(k):
+            ocopy(lax.rem(me + k, n_seq), me).wait_send()
+
+        @pl.loop(1, n_dev)
+        def _(k):
+            other = lax.rem(slot + k, n_dev)
+            rcopy(other, slot).wait_send()
+            rcopy(other, other).wait_recv()
 
     def compute(h):
         q = q_ref[pl.ds(h * width, width)].reshape(rows, dim)
@@ -230,8 +322,12 @@
             put(b, 1, dot(probs, do, 0, 0))
         out = out.astype(jnp.bfloat16)
         for w in range(width):
-            at = pl.ds(pl.multiple_of((h * width + w) * dim, dim), dim)
-            o_ref[:, at] = out[w * tok : (w + 1) * tok]
+            head = h * width + w
+            part = out[w * tok : (w + 1) * tok]
+            if relay:
+                send_out(head, part)
+            else:
+                o_ref[:, pl.ds(pl.multiple_of(head * dim, dim), dim)] = part
         delta = jnp.sum(do.astype(jnp.float32) * out.astype(jnp.float32), axis=1, keepdims=True)
         dq = jnp.zeros((rows, dim), jnp.float32)
         for b in range(5):
@@ -241,23 +337,25 @@
             put(b, 0, FACTOR * dot(ds, q, 0, 0))
         dq_ref[pl.ds(h * width, width)] = (FACTOR * dq).astype(jnp.bfloat16).reshape(width, tok, dim)
 
-    stage_z(0)
-    stage_z(1)
-    stage_x(0)
-    stage_c(0)
+    stage_z(turn(0, plane))
+    stage_z(turn(1, plane))
+    stage_x(turn(0, plane))
+    stage_c(turn(0, plane))
     masks()
 
     @pl.loop(0, heads)
-    def _(h):
-        @pl.when(h + 2 < heads)
-        def _():
-            stage_z(h + 2)
-
-        @pl.when(h + 1 < heads)
-        def _():
-            stage_x(h + 1)
-
-        @pl.when(h > 0)
+    def _(step):
+        h = turn(step, plane)
+
+        @pl.when(step + 2 < heads)
+        def _():
+            stage_z(turn(step + 2, plane))
+
+        @pl.when(step + 1 < heads)
+        def _():
+            stage_x(turn(step + 1, plane))
+
+        @pl.when(step > 0)
         def _():
             stage_c(h)
 
@@ -265,20 +363,23 @@
         gcopy(D, h, core_peer).start()
         gcopy(C, h, core_peer).start()
 
-        @pl.when(h >= 1)
-        def _():
-            grad_x(h - 1)
-
-        @pl.when(h >= 2)
-        def _():
-            grad_z(h - 2)
-
-    grad_x(heads - 1)
-    grad_z(heads - 2)
-    grad_z(heads - 1)
+        @pl.when(step >= 1)
+        def _():
+            grad_x(turn(step + heads - 1, plane))
+
+        @pl.when(step >= 2)
+        def _():
+            grad_z(turn(step + heads - 2, plane))
+
+    grad_x(turn(heads - 1, plane))
+    grad_z(turn(heads - 2, plane))
+    grad_z(turn(heads - 1, plane))
+    if relay:
+        pick_and_send()
 
     @pl.loop(0, heads)
-    def _(h):
+    def _(step):
+        h = turn(step, plane)
         finish(h)
 
         @pl.when(has_next)
@@ -296,20 +397,36 @@
         def _():
             gcopy(Z, h, me - 4).wait_send()
 
-
-def attention(q, do, seg, own):
+    if relay:
+        settle()
+
+
+def attention(q, do, seg, own, order, relay):
     heads, tok, dim = q.shape
     kv_heads, rows_kv, _ = own.shape
     width = heads // kv_heads
     pairs = heads * tok * tok * 5
     vmem = pl.BlockSpec(memory_space=pltpu.VMEM)
     grad = (kv_heads, 2 * tok, dim)
+    n_seq, n_head = lax.axis_size("seq"), lax.axis_size("head")
+    blocks = order.shape[0]
+    out_shape = (tok // n_head, n_head * heads * dim) if relay else (tok, heads * dim)
+    rows_out = tok * n_seq // blocks
+    relay_scratch = [
+        pltpu.VMEM((heads, blocks // n_seq, rows_out, dim), jnp.bfloat16),
+        pltpu.VMEM((n_seq, blocks // n_seq, rows_out, dim), jnp.bfloat16),
+        pltpu.VMEM((blocks, rows_out, dim), jnp.bfloat16),
+        pltpu.SemaphoreType.DMA((n_seq,)),
+        pltpu.SemaphoreType.DMA((n_seq,)),
+        pltpu.SemaphoreType.DMA((blocks,)),
+        pltpu.SemaphoreType.DMA((blocks,)),
+    ]
     return pl.pallas_call(
-        functools.partial(attention_kernel, lax.axis_size("seq")),
-        in_specs=[vmem] * 4,
+        functools.partial(attention_kernel, n_seq, n_head, relay),
+        in_specs=[vmem] * 4 + [pl.BlockSpec(memory_space=pltpu.SMEM)],
         out_specs=[vmem] * 3,
         out_shape=[
-            jax.ShapeDtypeStruct((tok, heads * dim), jnp.bfloat16),
+            jax.ShapeDtypeStruct(out_shape, jnp.bfloat16),
             jax.ShapeDtypeStruct((heads, tok, dim), jnp.bfloat16),
             jax.ShapeDtypeStruct(grad, jnp.bfloat16),
         ],
@@ -326,7 +443,8 @@
             pltpu.SemaphoreType.DMA((4, kv_heads)),
             pltpu.SemaphoreType.DMA((4, kv_heads)),
             pltpu.SemaphoreType.DMA((4, kv_heads)),
-        ],
+        ]
+        + (relay_scratch if relay else []),
         compiler_params=pltpu.CompilerParams(
             vmem_limit_bytes=48 * 2**20, collective_id=0, has_side_effects=True
         ),
@@ -334,7 +452,7 @@
             flops=10 * pairs * dim, bytes_accessed=8 * 2**20, transcendentals=pairs
         ),
         name="attention",
-    )(q, do, seg, own)
+    )(q, do, seg, own, order)
 
 
 def pick_kernel(order_ref, held_ref, out_ref):
@@ -371,9 +489,19 @@
         ],
         axis=1,
     )
+    relay = q_heads == seq_count and block_order.shape[0] == seq_count * head_count
     attended, dq, grads = attention(
-        jnp.moveaxis(queries, 1, 0), jnp.moveaxis(output_gradient, 1, 0), seg[:, None], own
+        jnp.moveaxis(queries, 1, 0),
+        jnp.moveaxis(output_gradient, 1, 0),
+        seg[:, None],
+        own,
+        block_order,
+        relay,
     )
+    grads = jnp.moveaxis(grads.reshape(kv_heads, 2, tok, dim), 0, 2)
+    dq = jnp.moveaxis(dq, 0, 1)
+    if relay:
+        return (attended, dq, grads[0], grads[1])
 
     nb = block_order.shape[0] // seq_count
     piece = tok // nb // seq_count
@@ -392,8 +520,7 @@
     halves = lax.all_to_all(reordered, "head", split_axis=0, concat_axis=0, tiled=True)
     relaid = jnp.swapaxes(halves, 0, 1).reshape(tok // head_count, head_count * features)
 
-    grads = jnp.moveaxis(grads.reshape(kv_heads, 2, tok, dim), 0, 2)
-    return (relaid, jnp.moveaxis(dq, 0, 1), grads[0], grads[1])
+    return (relaid, dq, grads[0], grads[1])
 
 
 def solution(mesh):

time: 159 us -> 116 us (0.73)
  blocking collectives: 60.3 us -> 0 us
  Pallas kernels: 71.1 us -> 104 us
  waiting for transfers between devices: 11.3 us -> 0 us
  starting transfers between devices: 3.58 us -> 0 us
    all_to_all x2 -> x0, blocking collectives: 60.3 us -> none  [the longest x1 30.5 us: local(): lax.all_to_all(flat, 'seq', split_axis=0, concat_axis=0, tiled=True)]
    pallas_call x2 -> x1, Pallas kernels: 71.1 us -> 104 us  [attention(): pl.pallas_call(functools.partial(attention_kernel, n_seq, n_head, relay),...]
    all_to_all x1 -> x0, waiting for transfers between devices: 11.3 us -> none  [local(): lax.all_to_all(reordered, 'head', split_axis=0, concat_axis=0, tiled=True)]
    all_to_all x1 -> x0, starting transfers between devices: 3.58 us -> none  [local(): lax.all_to_all(reordered, 'head', split_axis=0, concat_axis=0, tiled=True)]
    unnamed x6 -> x8, local copies, waits for them, and re-layouts: 3.25 us -> 3.61 us
  transfers between devices with their start and end apart: 1 -> 0, of which waited for: 1 -> 0; matrix products, arithmetic and copies ran while one was open for 2% -> 0% of each run, Pallas kernels for 0% -> 0%
where the time goes in v3:
time: 116 us; the launch traced here: 114 us
  Pallas kernels  104 us (90%)
  local copies, waits for them, and re-layouts  7.4 us (6%)
  other arithmetic  1.73 us (1%)
    pallas_call x1, Pallas kernels, attention(): pl.pallas_call(functools.partial(attention_kernel, n_seq, n_head, relay),...  104 us
    unnamed x8, local copies, waits for them, and re-layouts  3.61 us

profile of v3, /device:TPU:8, one launch (start us, length us, event | category | flops | bytes accessed | tf_op | source)
XLA Modules:
  0.0 114.1 jit_solution(16829910015473745588)
XLA Ops:
  0.6 0.7 convert_bitcast_fusion
  1.3 0.1 copy.20.seg_ref
  1.5 1.4 %copy_bitcast_fusion.3 = (bf16[8,256,128]{2,1,0:T(8,128)(2,1)S(1)}, bf16[8,256,128]{2,1,0:T(8,128)(2,1)S(1)}) fusion(bf16[256,8,128]{2,1,0:T(8,128)(2,1)} %param.8, bf16[256,8,128]{2,1,0:T(8,128)(2,1)} %param.7), kind=kLoop, calls=%fused_computation.6 | loop fusion | bytes 2097152 | tf_op jit(solution)/shard_map/transpose | solution.py:487
  2.9 0.0 copy-start.1
  2.9 0.0 copy-start.2
  2.9 1.0 pad_maximum_fusion.own_ref
  3.9 0.6 copy-done.1
  4.5 0.3 copy-done.2
  4.8 0.0 copy-start
  4.8 0.5 copy_bitcast_fusion.1
  5.4 0.1 copy-done
  5.5 104.3 %attention.1 = (bf16[128,4096]{1,0:T(8,128)(2,1)S(1)}, bf16[16,256,128]{2,1,0:T(8,128)(2,1)S(1)}, bf16[8,512,128]{2,1,0:T(8,128)(2,1)S(1)}) custom-call(bf16[16,256,128]{2,1,0:T(8,128)(2,1)S(1)} %get-tuple-element.25.q_ref, bf16[16,256,128]{2,1,0:T(8,128)(2,1)S(1)} %get-tuple-element.24.do_ref, f32[256,1]{1,0:T(8,128)S(1)} %copy.20.seg_ref, ...), custom_call_target="tpu_custom_call" | custom-call | flops 6710886400 | bytes 8388608 | tf_op jit(solution)/shard_map/attention/pallas_call | solution.py:424
  109.7 1.6 %copy.22 = bf16[256,16,128]{2,1,0:T(8,128)(2,1)} copy(bf16[256,16,128]{2,0,1:T(8,128)(2,1)S(1)} %bitcast.21) | data formatting | bytes 2097152
  111.4 0.7 copy.28
  112.1 1.0 slice_bitcast_fusion
  113.1 1.0 copy.30
  (2 shorter events, 0.0 us)
Async XLA Ops:
  2.9 1.6 %copy-start.1 = (bf16[256,16,128]{2,1,0:T(8,128)(2,1)S(1)}, bf16[256,16,128]{2,1,0:T(8,128)(2,1)}, u32[]{:S(2)}) copy-start(bf16[256,16,128]{2,1,0:T(8,128)(2,1)} %param.9) | copy-start | bytes 3145732
  2.9 1.9 %copy-start.2 = (bf16[256,16,128]{2,1,0:T(8,128)(2,1)S(1)}, bf16[256,16,128]{2,1,0:T(8,128)(2,1)}, u32[]{:S(2)}) copy-start(bf16[256,16,128]{2,1,0:T(8,128)(2,1)} %param.6) | copy-start | bytes 3145732
  4.8 0.7 copy-start

commit v4 on v3

--- a/solution.py
+++ b/solution.py
@@ -373,9 +373,9 @@
 
     grad_x(turn(heads - 1, plane))
     grad_z(turn(heads - 2, plane))
-    grad_z(turn(heads - 1, plane))
     if relay:
         pick_and_send()
+    grad_z(turn(heads - 1, plane))
 
     @pl.loop(0, heads)
     def _(step):

time: 116 us -> 116 us (level)
  no operation moved by 1% of the time
where the time goes in v4:
time: 116 us; the launch traced here: 114 us
  Pallas kernels  104 us (90%)
  local copies, waits for them, and re-layouts  7.4 us (6%)
  other arithmetic  1.73 us (1%)
    pallas_call x1, Pallas kernels, attention(): pl.pallas_call(functools.partial(attention_kernel, n_seq, n_head, relay),...  104 us
    unnamed x8, local copies, waits for them, and re-layouts  3.61 us

profile of v4, /device:TPU:8, one launch (start us, length us, event | category | flops | bytes accessed | tf_op | source)
XLA Modules:
  0.0 114.1 jit_solution(5973970012725992413)
XLA Ops:
  0.6 0.7 convert_bitcast_fusion
  1.3 0.1 copy.20.seg_ref
  1.5 1.4 %copy_bitcast_fusion.3 = (bf16[8,256,128]{2,1,0:T(8,128)(2,1)S(1)}, bf16[8,256,128]{2,1,0:T(8,128)(2,1)S(1)}) fusion(bf16[256,8,128]{2,1,0:T(8,128)(2,1)} %param.8, bf16[256,8,128]{2,1,0:T(8,128)(2,1)} %param.7), kind=kLoop, calls=%fused_computation.6 | loop fusion | bytes 2097152 | tf_op jit(solution)/shard_map/transpose | solution.py:487
  2.9 0.0 copy-start.1
  2.9 0.0 copy-start.2
  2.9 1.0 pad_maximum_fusion.own_ref
  3.9 0.6 copy-done.1
  4.5 0.3 copy-done.2
  4.8 0.0 copy-start
  4.8 0.5 copy_bitcast_fusion.1
  5.4 0.1 copy-done
  5.5 104.3 %attention.1 = (bf16[128,4096]{1,0:T(8,128)(2,1)S(1)}, bf16[16,256,128]{2,1,0:T(8,128)(2,1)S(1)}, bf16[8,512,128]{2,1,0:T(8,128)(2,1)S(1)}) custom-call(bf16[16,256,128]{2,1,0:T(8,128)(2,1)S(1)} %get-tuple-element.25.q_ref, bf16[16,256,128]{2,1,0:T(8,128)(2,1)S(1)} %get-tuple-element.24.do_ref, f32[256,1]{1,0:T(8,128)S(1)} %copy.20.seg_ref, ...), custom_call_target="tpu_custom_call" | custom-call | flops 6710886400 | bytes 8388608 | tf_op jit(solution)/shard_map/attention/pallas_call | solution.py:424
  109.8 1.6 %copy.22 = bf16[256,16,128]{2,1,0:T(8,128)(2,1)} copy(bf16[256,16,128]{2,0,1:T(8,128)(2,1)S(1)} %bitcast.21) | data formatting | bytes 2097152
  111.4 0.7 copy.28
  112.1 1.0 slice_bitcast_fusion
  113.1 1.0 copy.30
  (2 shorter events, 0.0 us)
Async XLA Ops:
  2.9 1.6 %copy-start.1 = (bf16[256,16,128]{2,1,0:T(8,128)(2,1)S(1)}, bf16[256,16,128]{2,1,0:T(8,128)(2,1)}, u32[]{:S(2)}) copy-start(bf16[256,16,128]{2,1,0:T(8,128)(2,1)} %param.9) | copy-start | bytes 3145732
  2.9 1.9 %copy-start.2 = (bf16[256,16,128]{2,1,0:T(8,128)(2,1)S(1)}, bf16[256,16,128]{2,1,0:T(8,128)(2,1)}, u32[]{:S(2)}) copy-start(bf16[256,16,128]{2,1,0:T(8,128)(2,1)} %param.6) | copy-start | bytes 3145732
  4.8 0.7 copy-start
